TPU v7x, 256 devices: a whole 4x4x8 slice. The times are simulated.
256 devices in a mesh: blk: 16 (over x_lo, z), red: 16 (over x_hi, y, core).
Axes of the slice: x: 4 (x_hi: 2, x_lo: 2; x = x_hi * 2 + x_lo), y: 4, z: 8, core: 2. Of those that a mesh axis runs over, the one named last changes fastest.
Arguments:
- resid: float32 [1024, 16384], P('blk', 'red'), may hold values from -64 to 64
- norm_gain: float32 [16384], P('red'), may hold values from 0.1 to 1.9
- w_query: bfloat16 [16384, 16384], P('red', 'blk'), may hold values from -0.046875 to 0.046875
- w_key: bfloat16 [16384, 1024], P('red'), may hold values from -0.046875 to 0.046875
- w_value: bfloat16 [16384, 1024], P('red'), may hold values from -0.046875 to 0.046875
- w_out: bfloat16 [16384, 16384], P('blk', 'red'), may hold values from -0.046875 to 0.046875
- cache_key: bfloat16 [8192, 1024], P('red'), may hold values from -512 to 512
- cache_value: bfloat16 [8192, 1024], P('red'), may hold values from -8 to 8
- prefix_len: int32 [1], replicated, may hold values from 4096 to 8192
Outputs:
- updated: float32 [1024, 16384], P('blk', 'red')
Inputs may be any that keep to these rules, and one draw needn't show every extreme that they name: `prefix_len`: cache slots below it hold the sequence's earlier tokens; the others are unused.
All inputs are finite; a program needn't handle non-finite values.
Results may differ from a plain program's by a relative error of at most 0.003.
The roundings to bfloat16 on the way count: a program that leaves them out, or rounds other values in their place, can miss the bound.
Values may be sent and summed in bfloat16 or wider, within the bound.
A program may use at most 192 MiB of HBM per device.

v0:
```python
import jax
import jax.numpy as jnp
from jax import lax
from jax.sharding import PartitionSpec as P

KV = 8
HD = 128


theta = 500000.0


def rotate(values, positions):
    half = values.shape[-1] // 2
    steps = jnp.arange(half, dtype=jnp.float32)
    freq = theta ** (-(steps * 2.0) / values.shape[-1])
    angle = positions.astype(jnp.float32)[:, None] * freq[None, :]
    cosine = jnp.cos(angle)[:, None, :]
    sine = jnp.sin(angle)[:, None, :]
    first = values[..., :half]
    second = values[..., half:]
    return jnp.concatenate(
        [first * cosine - second * sine, second * cosine + first * sine], axis=-1
    )


def finish(summed, positions, q_width):
    count = summed.shape[0]
    heads_here = q_width // HD
    query = rotate(summed[:, :q_width].reshape(count, heads_here, HD), positions).astype(
        jnp.bfloat16
    )
    key_new = (
        rotate(summed[:, q_width : q_width + HD].reshape(count, 1, HD), positions)
        .astype(jnp.bfloat16)
        .reshape(count, HD)
    )
    value_new = summed[:, q_width + HD :].astype(jnp.bfloat16)
    return (query, key_new, value_new)


def on_device(resid, norm_gain, w_query, w_key, w_value, w_out, cache_key, cache_value, prefix_len):
    blk_count = lax.axis_size("blk")
    red_count = lax.axis_size("red")
    blk_at = lax.axis_index("blk")
    red_at = lax.axis_index("red")
    total_sq = lax.psum(jnp.sum(resid * resid, axis=1), "red")
    features = resid.shape[1] * red_count
    normed = (resid * lax.rsqrt(total_sq[:, None] / features + 1e-05) * norm_gain[None, :]).astype(
        jnp.bfloat16
    )
    per_head = blk_count // KV
    head_at = blk_at // per_head
    my_wk = lax.dynamic_slice_in_dim(w_key, head_at * HD, HD, 1)
    my_wv = lax.dynamic_slice_in_dim(w_value, head_at * HD, HD, 1)
    joined = jnp.concatenate([w_query, my_wk, my_wv], axis=1)
    partial_proj = jnp.dot(
        lax.all_gather(normed, "blk", axis=0, tiled=True),
        joined,
        preferred_element_type=jnp.float32,
    )
    span = partial_proj.shape[0]
    rows = span // red_count
    q_width = w_query.shape[1]
    start = prefix_len[0]
    low = red_at * rows
    mine = lax.psum_scatter(partial_proj, "red", scatter_dimension=0, tiled=True)
    query, key_new, value_new = finish(
        mine, start + low + jnp.arange(rows, dtype=jnp.int32), q_width
    )
    my_ck = lax.dynamic_slice_in_dim(cache_key, head_at * HD, HD, 1)
    my_cv = lax.dynamic_slice_in_dim(cache_value, head_at * HD, HD, 1)
    c_rows = my_ck.shape[0]
    scale = HD ** (-0.5)
    every = jnp.arange(span, dtype=jnp.int32)
    fresh_k, fresh_v = (
        lax.all_gather(key_new, "red", axis=0, tiled=True),
        lax.all_gather(value_new, "red", axis=0, tiled=True),
    )
    all_ck, all_cv = (
        lax.all_gather(my_ck, "red", axis=0, tiled=True),
        lax.all_gather(my_cv, "red", axis=0, tiled=True),
    )
    cache_ok = (jnp.arange(c_rows * red_count, dtype=jnp.int32) < start)[None, None, :]
    here = low + jnp.arange(rows, dtype=jnp.int32)
    causal = (every[None, :] <= here[:, None])[:, None, :]
    old_scores = (
        jnp.einsum("tgd,cd->tgc", query, all_ck, preferred_element_type=jnp.float32) * scale
    )
    new_scores = (
        jnp.einsum("tgd,sd->tgs", query, fresh_k, preferred_element_type=jnp.float32) * scale
    )
    peak = jnp.maximum(
        jnp.max(jnp.where(cache_ok, old_scores, -1e30), axis=2),
        jnp.max(jnp.where(causal, new_scores, -1e30), axis=2),
    )
    old_w = jnp.where(cache_ok, jnp.exp(old_scores - peak[:, :, None]), 0.0).astype(jnp.bfloat16)
    new_w = jnp.where(causal, jnp.exp(new_scores - peak[:, :, None]), 0.0).astype(jnp.bfloat16)
    total = jnp.sum(old_w, axis=2, dtype=jnp.float32) + jnp.sum(new_w, axis=2, dtype=jnp.float32)
    mixed = jnp.einsum("tgc,cd->tgd", old_w, all_cv, preferred_element_type=jnp.float32)
    mixed = mixed + jnp.einsum("tgs,sd->tgd", new_w, fresh_v, preferred_element_type=jnp.float32)
    attention = (mixed / total[:, :, None]).astype(jnp.bfloat16).reshape(rows, q_width)
    out_terms = jnp.dot(
        lax.all_gather(attention, "red", axis=0, tiled=True),
        w_out,
        preferred_element_type=jnp.float32,
    )
    summed = lax.psum_scatter(out_terms, "blk", scatter_dimension=0, tiled=True)
    return resid + summed


def solution(mesh):
    placed = (
        P("blk", "red"),
        P("red"),
        P("red", "blk"),
        P("red", None),
        P("red", None),
        P("blk", "red"),
        P("red", None),
        P("red", None),
        P(),
    )
    return jax.shard_map(
        on_device, mesh=mesh, in_specs=placed, out_specs=P("blk", "red"), check_vma=False
    )
```

profile of v0, /device:TPU:32, one launch (start us, length us, event | category | flops | bytes accessed | tf_op | source)
XLA Modules:
  0.0 476.1 jit_solution(16847387863999591196)
XLA Ops:
  6.5 0.0 copy-start
  6.5 0.0 all-gather.5.cloned.1.call-start
  6.5 1.2 multiply_reduce_fusion
  7.8 38.1 %psum.7 = f32[64]{0:T(128)S(1)} all-reduce(f32[64]{0:T(128)S(1)} %multiply_reduce_fusion), channel_id=1, replica_groups=mesh['blk'=16,'red'=16] {'red'}, use_global_device_ids=true, to_apply=%region_1.0 | all-reduce | flops 64 | bytes 512 | tf_op jit(solution)/shard_map/psum | solution.py:47
  45.8 1.7 multiply_convert_fusion
  47.5 0.0 all-gather.5.cloned.1.call-update
  47.6 0.0 reduce-scatter.3.cloned.1.call-start
  47.6 1.1 constant_dynamic-slice_fusion.2
  48.7 67.5 %all-gather.5.cloned.1.call-done = bf16[1024,1024]{1,0:T(8,128)(2,1)} async-done(((bf16[64,1024]{1,0:T(8,128)(2,1)}), bf16[1024,1024]{1,0:T(8,128)(2,1)}) %all-gather.5.cloned.1.call-update) | async-done | bytes 2097168 | tf_op jit(solution)/shard_map/all_gather | solution.py:58
  116.3 7.4 %fusion = f32[1024,1280]{1,0:T(8,128)} fusion(bf16[1024,1024]{1,0:T(8,128)(2,1)} %all-gather.5.cloned.1.call-done, bf16[1024,128]{1,0:T(8,128)(2,1)S(1)} %get-tuple-element.15, bf16[1024,128]{1,0:T(8,128)(2,1)S(1)} %get-tuple-element.16, bf16[1024,1024]{1,0:T(8,128)(2,1)} %param.11), kind=kOutput, calls=%fused_computation.3 | convolution fusion | flops 2692218880 | bytes 9961472 | tf_op jit(solution)/shard_map/dot_general | solution.py:57
  123.7 0.0 reduce-scatter.3.cloned.1.call-update
  123.7 0.0 all-gather.7.cloned.1.call-start
  123.7 1.6 constant_dynamic-slice_fusion.1
  125.3 0.0 all-gather.7.cloned.1.call-update
  125.3 0.0 all-gather.9.cloned.1.call-start
  125.4 1.6 constant_dynamic-slice_fusion
  126.9 0.0 all-gather.9.cloned.1.call-update
  127.0 0.0 all-gather.11.cloned.1.call-start
  127.7 0.1 iota_compare_fusion
  127.8 0.2 multiply_cosine_fusion.1
  128.0 86.8 %reduce-scatter.3.cloned.1.call-done = f32[64,1280]{1,0:T(8,128)} async-done(((f32[1024,1280]{1,0:T(8,128)}), f32[64,1280]{1,0:T(8,128)}) %reduce-scatter.3.cloned.1.call-update) | async-done | bytes 327696 | tf_op jit(solution)/shard_map/reduce_scatter | solution.py:67
  214.8 1.0 slice_bitcast_fusion
  215.9 0.8 slice_bitcast_fusion.1
  216.6 0.2 fusion.24
  216.8 0.1 pad_maximum_fusion.3
  216.9 22.2 %all_gather.20 = bf16[1024,128]{1,0:T(8,128)(2,1)S(1)} all-gather(bf16[64,128]{1,0:T(8,128)(2,1)S(1)} %pad_maximum_fusion.3), channel_id=1, replica_groups=mesh['blk'=16,'red'=16] {'red'}, dimensions={0}, use_global_device_ids=true | all-gather | bytes 278528 | tf_op jit(solution)/shard_map/all_gather | solution.py:77
  239.1 0.2 subtract_convert_fusion
  239.2 2.0 select_reduce_fusion.1
  241.2 27.9 %all-gather.7.cloned.1.call-done = bf16[8192,128]{1,0:T(8,128)(2,1)} async-done(((bf16[512,128]{1,0:T(8,128)(2,1)}), bf16[8192,128]{1,0:T(8,128)(2,1)}) %all-gather.7.cloned.1.call-update) | async-done | bytes 2097168 | tf_op jit(solution)/shard_map/all_gather | solution.py:81
  269.1 8.9 %select_reduce_fusion = (f32[64,8]{1,0:T(8,128)S(1)}, f32[64,8,8192]{2,1,0:T(8,128)}) fusion(pred[8192]{0:T(1024)(128)(4,1)S(1)} %iota_compare_fusion.1, bf16[8192,128]{1,0:T(8,128)(2,1)} %all-gather.7.cloned.1.call-done, bf16[64,8,64]{2,1,0:T(8,128)(2,1)S(1)} %get-tuple-element.6, bf16[64,8,64]{2,1,0:T(8,128)(2,1)S(1)} %get-tuple-element.5), kind=kOutput, calls=%fused_computation.2 | convolution fusion | flops 1086586368 | bytes 19015680 | tf_op jit(solution)/shard_map/tgd,cd->tgc/dot_general | solution.py:88
  278.0 0.0 copy-done.1
  278.0 0.7 convert_reduce_fusion.1
  278.8 9.7 %convert_reduce_fusion = f32[64,8]{1,0:T(8,128)S(1)} fusion(f32[64,8]{1,0:T(8,128)S(1)} %max.7, f32[64,8,8192]{2,1,0:T(8,128)} %get-tuple-element.12, pred[8192]{0:T(1024)(128)(4,1)S(1)} %iota_compare_fusion.1), kind=kLoop, calls=%fused_computation | loop fusion | flops 25165312 | bytes 16789504 | tf_op jit(solution)/shard_map/reduce_sum | solution.py:99
  288.5 0.8 slice.55
  289.3 22.1 %all_gather.22 = bf16[1024,128]{1,0:T(8,128)(2,1)S(1)} all-gather(bf16[64,128]{1,0:T(8,128)(2,1)S(1)} %slice.55), channel_id=1, replica_groups=mesh['blk'=16,'red'=16] {'red'}, dimensions={0}, use_global_device_ids=true | all-gather | bytes 278528 | tf_op jit(solution)/shard_map/all_gather | solution.py:78
  311.4 11.8 %all-gather.9.cloned.1.call-done = bf16[8192,128]{1,0:T(8,128)(2,1)} async-done(((bf16[512,128]{1,0:T(8,128)(2,1)}), bf16[8192,128]{1,0:T(8,128)(2,1)}) %all-gather.9.cloned.1.call-update) | async-done | bytes 2097168 | tf_op jit(solution)/shard_map/all_gather | solution.py:82
  323.2 7.9 %fusion.6 = f32[64,8,128]{2,1,0:T(8,128)S(1)} fusion(bf16[8192,128]{1,0:T(8,128)(2,1)} %all-gather.9.cloned.1.call-done, f32[64,8,8192]{2,1,0:T(8,128)} %get-tuple-element.12, f32[64,8]{1,0:T(8,128)S(1)} %max.7, pred[8192]{0:T(1024)(128)(4,1)S(1)} %iota_compare_fusion.1), kind=kOutput, calls=%fused_computation.9 | convolution fusion | flops 1090519040 | bytes 19146752 | tf_op jit(solution)/shard_map/tgc,cd->tgd/dot_general | solution.py:100
  331.1 0.0 copy-done.2
  331.1 0.7 fusion.11
  331.8 0.7 copy.13
  332.5 0.0 all-gather.11.cloned.1.call-update
  332.5 0.0 reduce-scatter.5.cloned.1.call-start
  332.6 51.6 %all-gather.11.cloned.1.call-done = bf16[1024,1024]{1,0:T(8,128)(2,1)} async-done(((bf16[64,1024]{1,0:T(8,128)(2,1)}), bf16[1024,1024]{1,0:T(8,128)(2,1)}) %all-gather.11.cloned.1.call-update) | async-done | bytes 2097168 | tf_op jit(solution)/shard_map/all_gather | solution.py:104
  384.1 0.0 copy-done
  384.2 5.9 %fusion.30 = f32[1024,1024]{1,0:T(8,128)} fusion(bf16[1024,1024]{1,0:T(8,128)(2,1)} %all-gather.11.cloned.1.call-done, bf16[1024,1024]{1,0:T(8,128)(2,1)S(1)} %copy-done), kind=kOutput, calls=%fused_computation.61 | convolution fusion | flops 2147483648 | bytes 8388608 | tf_op jit(solution)/shard_map/dot_general | solution.py:103
  390.0 0.0 reduce-scatter.5.cloned.1.call-update
  390.0 77.5 %reduce-scatter.5.cloned.1.call-done = f32[64,1024]{1,0:T(8,128)} async-done(((f32[1024,1024]{1,0:T(8,128)}), f32[64,1024]{1,0:T(8,128)}) %reduce-scatter.5.cloned.1.call-update) | async-done | bytes 262160 | tf_op jit(solution)/shard_map/reduce_scatter | solution.py:108
  467.6 1.7 add.74
  (12 shorter events, 0.1 us)
Async XLA Ops:
  6.5 377.6 %copy-start = (bf16[1024,1024]{1,0:T(8,128)(2,1)S(1)}, bf16[1024,1024]{1,0:T(8,128)(2,1)}, u32[]{:S(2)}) copy-start(bf16[1024,1024]{1,0:T(8,128)(2,1)} %param.14) | copy-start | bytes 6291460
  6.5 109.7 %all-gather.5.cloned.1.call-start = ((), (), s32[]{:S(2)}) async-start(), calls=%async_computation.2 | async-start | bytes 2228224 | tf_op jit(solution)/shard_map/all_gather | solution.py:58
  47.6 167.3 %reduce-scatter.3.cloned.1.call-start = ((), (), s32[]{:S(2)}) async-start(), calls=%async_computation.3 | async-start | bytes 5570560 | tf_op jit(solution)/shard_map/reduce_scatter | solution.py:67
  123.7 145.5 %all-gather.7.cloned.1.call-start = ((), (), s32[]{:S(2)}) async-start(), calls=%async_computation.4 | async-start | bytes 2228224 | tf_op jit(solution)/shard_map/all_gather | solution.py:81
  125.3 197.9 %all-gather.9.cloned.1.call-start = ((), (), s32[]{:S(2)}) async-start(), calls=%async_computation.5 | async-start | bytes 2228224 | tf_op jit(solution)/shard_map/all_gather | solution.py:82
  127.0 257.2 %all-gather.11.cloned.1.call-start = ((), (), s32[]{:S(2)}) async-start(), calls=%async_computation.6 | async-start | bytes 2228224 | tf_op jit(solution)/shard_map/all_gather | solution.py:104
  269.1 8.9 %copy-start.1 = (f32[64,8,1024]{2,1,0:T(8,128)S(1)}, f32[64,8,1024]{2,1,0:T(8,128)}, u32[]{:S(2)}) copy-start(f32[64,8,1024]{2,1,0:T(8,128)} %get-tuple-element.14) | copy-start | bytes 6291460
  323.2 7.9 %copy-start.2 = (f32[64,8,1024]{2,1,0:T(8,128)S(1)}, f32[64,8,1024]{2,1,0:T(8,128)}, u32[]{:S(2)}) copy-start(f32[64,8,1024]{2,1,0:T(8,128)} %get-tuple-element.14) | copy-start | bytes 6291460
  332.5 135.0 %reduce-scatter.5.cloned.1.call-start = ((), (), s32[]{:S(2)}) async-start(), calls=%async_computation.7 | async-start | bytes 4456448 | tf_op jit(solution)/shard_map/reduce_scatter | solution.py:108
  390.0 77.5 %copy-start.3 = (f32[64,1024]{1,0:T(8,128)S(1)}, f32[64,1024]{1,0:T(8,128)}, u32[]{:S(2)}) copy-start(f32[64,1024]{1,0:T(8,128)} %param.9) | copy-start | bytes 786436
Sparse Core Ops, SparseCore 0:
  47.7 68.5 all-gather.4
  123.8 90.9 reduce-scatter.2
  217.6 51.4 all-gather.6
  271.8 51.4 all-gather.8
  332.6 51.4 all-gather.10
  390.2 77.3 reduce-scatter.4
where the time goes:
time: 479 us; the launch traced here: 476 us
  waiting for transfers between devices  323 us (67%)
  blocking collectives  82.4 us (17%)
  matrix products  32.6 us (7%)
  other arithmetic  15.9 us (3%)
  between operations  14.3 us (3%)
  local copies, waits for them, and re-layouts  7.46 us (2%)
    reduce_scatter x1, waiting for transfers between devices, on_device(): lax.psum_scatter(partial_proj, 'red', scatter_dimension=0, tiled=True)  86.8 us
    reduce_scatter x1, waiting for transfers between devices, on_device(): summed = lax.psum_scatter(out_terms, 'blk', scatter_dimension=0, tiled=True)  77.5 us
    all_gather x1, waiting for transfers between devices, on_device(): lax.all_gather(normed, 'blk', axis=0, tiled=True)  67.5 us
    all_gather x1, waiting for transfers between devices, on_device(): lax.all_gather(attention, 'red', axis=0, tiled=True)  51.6 us
    psum x1, blocking collectives, on_device(): total_sq = lax.psum(jnp.sum(resid * resid, axis=1), 'red')  38.1 us
    all_gather x1, waiting for transfers between devices, on_device(): lax.all_gather(my_ck, 'red', axis=0, tiled=True)  27.9 us
    all_gather x1, blocking collectives, on_device(): lax.all_gather(key_new, 'red', axis=0, tiled=True)  22.2 us
    all_gather x1, blocking collectives, on_device(): lax.all_gather(value_new, 'red', axis=0, tiled=True)  22.1 us
  transfers between devices with their start and end apart: 6, of which 6 were waited for; matrix products, arithmetic and copies ran while one was open for 6% of the time, Pallas kernels for 0%

commit v1 on v0

v1 whole, which is shorter than its diff:
```python
import functools
import math

import jax
import jax.numpy as jnp
from jax import lax
from jax.experimental import pallas as pl
from jax.experimental.pallas import tpu as pltpu
from jax.sharding import PartitionSpec as P

MESH = pl.DeviceIdType.MESH
F32, BF16, I16, I32 = jnp.float32, jnp.bfloat16, jnp.int16, jnp.int32

HD = 128
THETA = 500000.0
ROWS = 64
WIDE = 1024
PROJ = WIDE + 2 * HD
SLOTS = 512
CACHE = 8192
SPAN = 1024
KEYS = CACHE + SPAN
CHUNK = 1024
HALF = 256
STEP = 8.0
TOP = 32000.0
NEG = -1e30


def rem(a, n):
    return lax.rem(a, jnp.int32(n))


def quantize(dst, v):
    n = v.shape[1]
    fold = jnp.abs(v[:, :HD])
    for k in range(1, n // HD):
        fold = jnp.maximum(fold, jnp.abs(v[:, k * HD : (k + 1) * HD]))
    top = jnp.max(fold, axis=1, keepdims=True)
    e = jnp.ceil(jnp.log2(jnp.maximum(top, 1e-30)) * STEP)
    e = jnp.broadcast_to(e, (v.shape[0], HD))
    up = jnp.exp2(e * (-1.0 / STEP)) * TOP
    for k in range(n // HD):
        dst[:, k * HD : (k + 1) * HD] = jnp.round(v[:, k * HD : (k + 1) * HD] * up).astype(I32).astype(I16)
    dst[:, n : n + HD] = e.astype(I32).astype(I16)


def restore(src, n):
    e = src[:, n : n + HD].astype(I32).astype(F32)
    down = jnp.exp2(e * (1.0 / STEP)) * (1.0 / TOP)
    return jnp.concatenate(
        [src[:, k * HD : (k + 1) * HD].astype(I32).astype(F32) * down for k in range(n // HD)], axis=1
    )


def kernel(
    start_ref, resid_hbm, gain_ref, wq_hbm, wk_hbm, wv_hbm, wo_hbm, ck_hbm, cv_hbm, cos_ref, sin_ref,
    out_ref,
    res, w, wo, g, kv, pb, sq, pp, sib, qs, qr, acc, qh, s_ref, mix, att, op, xs, xr, zs, zr,
    load_sem, sq_send, sq_recv, ag_send, ag_recv, kv_send, kv_recv, sib_send, sib_recv, qs_send, qr_recv,
    nk_send, nk_recv, at_send, at_recv, xs_send, xr_recv, zs_send, zr_recv,
):
    b = lax.axis_index("blk")
    r = lax.axis_index("red")
    xl, z = lax.div(b, jnp.int32(8)), rem(b, 8)
    xh, y, c = lax.div(r, jnp.int32(8)), rem(lax.div(r, jnp.int32(2)), 4), rem(r, 2)
    chip = lax.div(r, jnp.int32(2))
    head = lax.div(b, jnp.int32(2))

    def blk_of(px, pz):
        return px * 8 + rem(pz + 16, 8)

    def red_of(px, py, pc):
        return (px * 4 + rem(py + 8, 4)) * 2 + pc

    z_up, z_down = (blk_of(xl, z + 1), r), (blk_of(xl, z - 1), r)
    x_pair = (blk_of(1 - xl, z), r)
    x_across = (blk_of(1 - xl, z), red_of(1 - xh, y, c))
    sibling = (b, red_of(xh, y, 1 - c))

    barrier = pltpu.get_barrier_semaphore()
    peers = [(b, rem(r + i, 16)) for i in range(1, 16)] + [z_up, z_down, x_pair, x_across]
    for p in peers:
        pl.semaphore_signal(barrier, inc=1, device_id=p, device_id_type=MESH)

    mine = pl.ds(pl.multiple_of(r * SLOTS, SLOTS), SLOTS)
    my_cols = pl.ds(pl.multiple_of(head * HD, HD), HD)
    pair_head = lax.div(blk_of(1 - xl, z), jnp.int32(2))
    pair_cols = pl.ds(pl.multiple_of(pair_head * HD, HD), HD)
    loads = [
        pltpu.make_async_copy(resid_hbm, res, load_sem.at[0]),
        pltpu.make_async_copy(ck_hbm.at[:, my_cols], kv.at[mine, 0:HD], load_sem.at[1]),
        pltpu.make_async_copy(cv_hbm.at[:, my_cols], kv.at[mine, HD : 2 * HD], load_sem.at[2]),
        pltpu.make_async_copy(ck_hbm.at[:, pair_cols], pb.at[:, 0:HD], load_sem.at[3]),
        pltpu.make_async_copy(cv_hbm.at[:, pair_cols], pb.at[:, HD : 2 * HD], load_sem.at[4]),
        pltpu.make_async_copy(wq_hbm, w.at[:, 0:WIDE], load_sem.at[5]),
        pltpu.make_async_copy(wk_hbm.at[:, my_cols], w.at[:, WIDE : WIDE + HD], load_sem.at[6]),
        pltpu.make_async_copy(wv_hbm.at[:, my_cols], w.at[:, WIDE + HD : PROJ], load_sem.at[7]),
        pltpu.make_async_copy(wo_hbm, wo, load_sem.at[8]),
    ]
    for cp in loads:
        cp.start()

    sends = []

    def send(src, dst, ssem, rsem, to):
        cp = pltpu.make_async_remote_copy(
            src_ref=src, dst_ref=dst, send_sem=ssem, recv_sem=rsem, device_id=to, device_id_type=MESH
        )
        cp.start()
        sends.append(cp)

    def arrived(dst, rsem):
        pltpu.make_async_remote_copy(
            src_ref=dst, dst_ref=dst, send_sem=load_sem.at[0], recv_sem=rsem, device_id=sibling, device_id_type=MESH
        ).wait_recv()

    loads[0].wait()
    fold = jnp.zeros((ROWS, HD), F32)
    for k in range(WIDE // HD):
        v = res[:, k * HD : (k + 1) * HD]
        fold = fold + v * v
    square = jnp.concatenate([fold, jnp.zeros((HD - ROWS, HD), F32)], axis=0).T
    sq[r] = jnp.broadcast_to(jnp.sum(square, axis=0, keepdims=True), (8, HD))
    pl.semaphore_wait(barrier, len(peers))
    for i in range(1, 16):
        send(sq.at[r], sq.at[r], sq_send.at[i], sq_recv.at[r], (b, rem(r + i, 16)))

    for cp in loads[1:5]:
        cp.wait()

    def kv_rows(red):
        return kv.at[pl.ds(pl.multiple_of(red * SLOTS, SLOTS), SLOTS), 0 : 2 * HD]

    kv_count = [0]

    def kv_send_to(red, to, src=None):
        send(kv_rows(red) if src is None else src, kv_rows(red), kv_send.at[kv_count[0]], kv_recv.at[red], to)
        kv_count[0] += 1

    kv_send_to(r, x_across, src=pb)
    for d in (1, 3, 2):
        kv_send_to(r, (b, red_of(xh, y + d, c)))
    kv_send_to(r, sibling)

    kv[:, 2 * HD : 3 * HD] = jnp.ones((KEYS, HD), BF16)

    for i in range(1, 16):
        p = rem(r + i, 16)
        arrived(sq.at[p], sq_recv.at[p])
    total = jnp.sum(sq[...], axis=0)[0:1]
    column = jnp.broadcast_to(total, (HD, HD)).T[:ROWS]
    factor = lax.rsqrt(column / (WIDE * 16.0) + 1e-05)
    for k in range(WIDE // HD):
        lanes = slice(k * HD, (k + 1) * HD)
        g[b, :, lanes] = (res[:, lanes] * factor * gain_ref[:, lanes]).astype(BF16)

    ag_count = [0]

    def g_send(px, pz, to):
        slot = blk_of(px, pz)
        send(g.at[slot], g.at[slot], ag_send.at[ag_count[0]], ag_recv.at[slot], to)
        ag_count[0] += 1

    def g_wait(px, pz):
        slot = blk_of(px, pz)
        arrived(g.at[slot], ag_recv.at[slot])

    ox = 1 - xl
    g_send(xl, z, z_up)
    g_send(xl, z, z_down)
    g_send(xl, z, x_pair)
    g_wait(ox, z)
    g_send(ox, z, z_up)
    g_send(ox, z, z_down)
    g_wait(xl, z - 1)
    g_send(xl, z - 1, z_up)
    g_wait(xl, z + 1)
    g_send(xl, z + 1, z_down)
    r_across = red_of(1 - xh, y, c)
    arrived(kv_rows(r_across), kv_recv.at[r_across])
    for d in (1, 3, 2):
        kv_send_to(r_across, (b, red_of(xh, y + d, c)))
    kv_send_to(r_across, sibling)
    g_wait(ox, z - 1)
    g_send(ox, z - 1, z_up)
    g_wait(ox, z + 1)
    g_send(ox, z + 1, z_down)
    g_wait(xl, z - 2)
    g_send(xl, z - 2, z_up)
    g_wait(xl, z + 2)
    g_send(xl, z + 2, z_down)
    for d in (1, 3):
        red = red_of(xh, y + d, c)
        arrived(kv_rows(red), kv_recv.at[red])
        kv_send_to(red, sibling)
    g_wait(xl, z - 3)
    g_send(xl, z - 3, z_up)
    g_send(xl, z - 3, x_pair)
    g_wait(xl, z + 3)
    g_send(xl, z + 3, x_pair)
    g_wait(ox, z - 2)
    g_wait(ox, z + 2)
    g_wait(xl, z - 4)
    g_send(xl, z - 4, x_pair)
    g_wait(ox, z - 3)
    g_wait(ox, z + 3)
    g_wait(ox, z - 4)

    for cp in loads[5:8]:
        cp.wait()

    def to_sibling(i):
        return pltpu.make_async_remote_copy(
            src_ref=pp.at[i, 1 - c], dst_ref=sib.at[i], send_sem=sib_send.at[i], recv_sem=sib_recv.at[i],
            device_id=sibling, device_id_type=MESH,
        )

    def to_chip(i):
        j = rem(chip + 1 + i, 8)
        return pltpu.make_async_remote_copy(
            src_ref=qs.at[i], dst_ref=qr.at[chip], send_sem=qs_send.at[i], recv_sem=qr_recv.at[chip],
            device_id=(b, j * 2 + c), device_id_type=MESH,
        )

    def pass_on(i):
        to_sibling(i).wait_recv()
        quantize(qs.at[i], pp[i, c] + sib[i])
        to_chip(i).start()

    def project(i, _):
        j = rem(chip + 1 + i, 8)
        x = g[pl.ds(j * 2, 2)].reshape(2 * ROWS, WIDE)
        for n in range(PROJ // 256):
            t = jnp.dot(x, w[:, n * 256 : (n + 1) * 256], preferred_element_type=F32)
            pp[i, :, :, n * 256 : (n + 1) * 256] = t.reshape(2, ROWS, 256)
        to_sibling(i).start()

        @pl.when(i > 0)
        def _():
            pass_on(i - 1)

        return 0

    lax.fori_loop(0, 8, project, 0)

    for red in (
        red_of(xh, y + 2, c), red_of(1 - xh, y + 1, c), red_of(1 - xh, y + 3, c), red_of(1 - xh, y + 2, c),
    ):
        arrived(kv_rows(red), kv_recv.at[red])
        kv_send_to(red, sibling)

    to_sibling(7).wait_recv()
    acc[...] = pp[7, c] + sib[7]
    for k in range(1, 8):
        p = rem(chip + k, 8)
        arrived(qr.at[p], qr_recv.at[p])
        acc[...] += restore(qr.at[p], PROJ)

    def turn(v):
        return (v * cos_ref[...] + pltpu.roll(v, HD // 2, 1) * sin_ref[...]).astype(BF16)

    fresh = pl.ds(pl.multiple_of(CACHE + r * ROWS, ROWS), ROWS)
    kv[fresh, 0:HD] = turn(acc[:, WIDE : WIDE + HD])
    kv[fresh, HD : 2 * HD] = acc[:, WIDE + HD : PROJ].astype(BF16)

    def nk_rows(red):
        return kv.at[pl.ds(pl.multiple_of(CACHE + red * ROWS, ROWS), ROWS), 0 : 2 * HD]

    def nk_to(slot, red, to):
        send(nk_rows(red), nk_rows(red), nk_send.at[slot], nk_recv.at[red], to)

    for k in range(1, 8):
        nk_to(k, r, (b, rem(chip + k, 8) * 2 + c))
    nk_to(0, r, sibling)
    for h in range(8):
        qh[h * ROWS : (h + 1) * ROWS, :] = turn(acc[:, h * HD : (h + 1) * HD])

    for k in range(8):
        red = rem(chip + k, 8) * 2 + 1 - c
        arrived(kv_rows(red), kv_recv.at[red])
    start = start_ref[0]
    turn_log = HD ** (-0.5) * math.log2(math.e)

    def scores(half, n):
        keys = kv[pl.ds(pl.multiple_of(n * CHUNK, CHUNK), CHUNK), 0:HD]
        return lax.dot_general(
            qh[half * HALF : (half + 1) * HALF, :], keys, (((1,), (1,)), ((), ())), preferred_element_type=F32
        )

    def keep(n, t, top):
        s_ref[:, pl.ds(pl.multiple_of(n * CHUNK, CHUNK), CHUNK)] = t
        for k in range(CHUNK // HD):
            top = jnp.maximum(top, t[:, k * HD : (k + 1) * HD])
        return top

    at_count = [0]

    def at_to(half, red, to):
        send(att.at[half, red], att.at[half, red], at_send.at[at_count[0]], at_recv.at[half, red], to)
        at_count[0] += 1

    for half in range(2):
        def plain(n, top, half=half):
            return keep(n, scores(half, n), top)

        def partly(n, top, half=half):
            slot = n * CHUNK + lax.broadcasted_iota(I32, (1, CHUNK), 1)
            return keep(n, scores(half, n) + jnp.where(slot < start, 0.0, NEG), top)

        top = jnp.full((HALF, HD), NEG, F32)
        top = lax.fori_loop(0, 4, plain, top)
        top = lax.fori_loop(4, 8, partly, top)
        if half == 0:
            for k in range(1, 8):
                red = rem(chip + k, 8) * 2 + c
                arrived(nk_rows(red), nk_recv.at[red])
                nk_to(7 + k, red, sibling)
            for k in range(8):
                red = rem(chip + k, 8) * 2 + 1 - c
                arrived(nk_rows(red), nk_recv.at[red])
        token = r * ROWS + rem(lax.broadcasted_iota(I32, (HALF, CHUNK), 0), ROWS)
        ahead = lax.broadcasted_iota(I32, (HALF, CHUNK), 1) > token
        top = keep(8, jnp.where(ahead, NEG, scores(half, 8)), top)
        peak = jnp.broadcast_to(jnp.max(top, axis=1, keepdims=True), (HALF, HD))

        mix[...] = jnp.zeros_like(mix)

        def weigh(n, _):
            base = n * CHUNK
            parts = []
            for k in range(CHUNK // HD):
                t = s_ref[:, pl.ds(pl.multiple_of(base + k * HD, HD), HD)]
                parts.append(jnp.exp2((t - peak) * turn_log).astype(BF16))
            wts = jnp.concatenate(parts, axis=1)
            vals = kv[pl.ds(pl.multiple_of(base, CHUNK), CHUNK), HD : 3 * HD]
            mix[...] += jnp.dot(wts, vals, preferred_element_type=F32)
            return 0

        lax.fori_loop(0, 9, weigh, 0)
        done = (mix[:, 0:HD] / mix[:, HD : 2 * HD]).astype(BF16)
        for h in range(4):
            att[half, r, :, h * HD : (h + 1) * HD] = done[h * ROWS : (h + 1) * ROWS, :]
        for k in range(1, 8):
            at_to(half, r, (b, rem(chip + k, 8) * 2 + c))
        at_to(half, r, sibling)

    for half in range(2):
        for k in range(1, 8):
            red = rem(chip + k, 8) * 2 + c
            arrived(att.at[half, red], at_recv.at[half, red])
            at_to(half, red, sibling)
    for half in range(2):
        for k in range(8):
            red = rem(chip + k, 8) * 2 + 1 - c
            arrived(att.at[half, red], at_recv.at[half, red])

    loads[8].wait()
    own = lambda d: blk_of(xl, z + d)
    other = lambda d: blk_of(ox, z + d)

    def project_out(slots):
        left = jnp.concatenate([att[0, s] for s in slots], axis=0)
        right = jnp.concatenate([att[1, s] for s in slots], axis=0)
        for n in range(WIDE // 256):
            lanes = slice(n * 256, (n + 1) * 256)
            t = jnp.dot(left, wo[0 : WIDE // 2, lanes], preferred_element_type=F32)
            t = t + jnp.dot(right, wo[WIDE // 2 : WIDE, lanes], preferred_element_type=F32)
            for k, s in enumerate(slots):
                op[s, :, lanes] = t[k * ROWS : (k + 1) * ROWS]

    def x_send(k, v):
        quantize(xs.at[k], v)
        send(xs.at[k], xr.at[k], xs_send.at[k], xr_recv.at[k], x_pair)

    def x_get(k):
        arrived(xr.at[k], xr_recv.at[k])
        return restore(xr.at[k], WIDE)

    def z_send(k, v, to):
        quantize(zs.at[k], v)
        send(zs.at[k], zr.at[k], zs_send.at[k], zr_recv.at[k], to)

    def z_get(k):
        arrived(zr.at[k], zr_recv.at[k])
        return restore(zr.at[k], WIDE)

    project_out([other(4), other(-3), other(2), other(-2)])
    x_send(0, op[other(4)])
    z_send(4, op[other(2)], z_up)
    z_send(9, op[other(-2)], z_down)
    x_send(1, op[other(-3)])
    project_out([own(4), own(-3), other(3), own(3)])
    x_send(2, op[other(3)])
    z_send(0, op[own(4)] + x_get(0), z_up)
    z_send(6, op[own(-3)] + x_get(1), z_down)
    project_out([other(1), other(-1), own(2), own(-2)])
    z_send(5, op[other(1)] + z_get(4), z_up)
    z_send(10, op[other(-1)] + z_get(9), z_down)
    project_out([own(1), own(-1), own(0), other(0)])
    z_send(1, op[own(3)] + z_get(0) + x_get(2), z_up)
    z_send(7, op[own(-2)] + z_get(6), z_down)
    x_send(3, op[other(0)] + z_get(5) + z_get(10))
    z_send(2, op[own(2)] + z_get(1), z_up)
    z_send(8, op[own(-1)] + z_get(7), z_down)
    z_send(3, op[own(1)] + z_get(2), z_up)
    out_ref[...] = res[...] + (op[own(0)] + x_get(3) + z_get(8) + z_get(3))

    for cp in sends:
        cp.wait_send()

    def drain(i, _):
        to_sibling(i).wait_send()

        @pl.when(i < 7)
        def _():
            to_chip(i).wait_send()

        return 0

    lax.fori_loop(0, 8, drain, 0)


def on_device(resid, norm_gain, w_query, w_key, w_value, w_out, cache_key, cache_value, prefix_len):
    r = lax.axis_index("red")
    half = HD // 2
    steps = jnp.arange(half, dtype=F32)
    freq = THETA ** (-(steps * 2.0) / HD)
    positions = prefix_len[0] + r * ROWS + jnp.arange(ROWS, dtype=I32)
    angle = positions.astype(F32)[:, None] * freq[None, :]
    cosine, sine = jnp.cos(angle), jnp.sin(angle)
    cosine = jnp.concatenate([cosine, cosine], axis=1)
    sine = jnp.concatenate([-sine, sine], axis=1)
    vmem = pl.BlockSpec(memory_space=pltpu.VMEM)
    hbm = pl.BlockSpec(memory_space=pl.ANY)
    dma = pltpu.SemaphoreType.DMA
    scratch = [
        pltpu.VMEM((ROWS, WIDE), F32),
        pltpu.VMEM((WIDE, PROJ), BF16),
        pltpu.VMEM((WIDE, WIDE), BF16),
        pltpu.VMEM((16, ROWS, WIDE), BF16),
        pltpu.VMEM((KEYS, 3 * HD), BF16),
        pltpu.VMEM((SLOTS, 2 * HD), BF16),
        pltpu.VMEM((16, 8, HD), F32),
        pltpu.VMEM((8, 2, ROWS, PROJ), F32),
        pltpu.VMEM((8, ROWS, PROJ), F32),
        pltpu.VMEM((8, ROWS, PROJ + HD), I16),
        pltpu.VMEM((8, ROWS, PROJ + HD), I16),
        pltpu.VMEM((ROWS, PROJ), F32),
        pltpu.VMEM((8 * ROWS, HD), BF16),
        pltpu.VMEM((HALF, KEYS), F32),
        pltpu.VMEM((HALF, 2 * HD), F32),
        pltpu.VMEM((2, 16, ROWS, WIDE // 2), BF16),
        pltpu.VMEM((16, ROWS, WIDE), F32),
        pltpu.VMEM((4, ROWS, WIDE + HD), I16),
        pltpu.VMEM((4, ROWS, WIDE + HD), I16),
        pltpu.VMEM((11, ROWS, WIDE + HD), I16),
        pltpu.VMEM((11, ROWS, WIDE + HD), I16),
        dma((9,)), dma((16,)), dma((16,)),
        dma((15,)), dma((16,)),
        dma((15,)), dma((16,)),
        dma((8,)), dma((8,)), dma((8,)), dma((8,)),
        dma((15,)), dma((16,)),
        dma((30,)), dma((2, 16)),
        dma((4,)), dma((4,)), dma((11,)), dma((11,)),
    ]
    return pl.pallas_call(
        kernel,
        out_shape=jax.ShapeDtypeStruct((ROWS, WIDE), F32),
        in_specs=[pl.BlockSpec(memory_space=pltpu.SMEM), hbm, vmem, hbm, hbm, hbm, hbm, hbm, hbm, vmem, vmem],
        out_specs=vmem,
        scratch_shapes=scratch,
        compiler_params=pltpu.CompilerParams(
            collective_id=0, has_side_effects=True, vmem_limit_bytes=58 * 1024 * 1024
        ),
    )(prefix_len, resid, norm_gain[None, :], w_query, w_key, w_value, w_out, cache_key, cache_value, cosine, sine)


def solution(mesh):
    placed = (
        P("blk", "red"), P("red"), P("red", "blk"), P("red", None), P("red", None), P("blk", "red"),
        P("red", None), P("red", None), P(),
    )
    return jax.shard_map(on_device, mesh=mesh, in_specs=placed, out_specs=P("blk", "red"), check_vma=False)
```

time: 479 us -> 131 us (0.27)
  waiting for transfers between devices: 323 us -> 0 us
  Pallas kernels: 0 us -> 128 us
  blocking collectives: 82.4 us -> 0 us
  matrix products: 32.6 us -> 0 us
  other arithmetic: 15.9 us -> 0.92 us
  between operations: 14.3 us -> 0.68 us
  local copies, waits for them, and re-layouts: 7.46 us -> 1.67 us
    reduce_scatter x2 -> x0, waiting for transfers between devices: 164 us -> none  [the longest x1 86.8 us: on_device(): lax.psum_scatter(partial_proj, 'red', scatter_dimension=0, tiled=True)]
    all_gather x4 -> x0, waiting for transfers between devices: 159 us -> none  [the longest x1 67.5 us: on_device(): lax.all_gather(normed, 'blk', axis=0, tiled=True)]
    pallas_call x0 -> x1, Pallas kernels: none -> 128 us  [on_device(): pl.pallas_call(kernel, out_shape=jax.ShapeDtypeStruct((ROWS, WIDE), F32),...]
    all_gather x2 -> x0, blocking collectives: 44.3 us -> none  [the longest x1 22.2 us: on_device(): lax.all_gather(key_new, 'red', axis=0, tiled=True)]
    psum x1 -> x0, blocking collectives: 38.1 us -> none  [on_device(): total_sq = lax.psum(jnp.sum(resid * resid, axis=1), 'red')]
    dot_general x6 -> x0, matrix products: 32.6 us -> none  [the longest x1 8.87 us: on_device(): jnp.einsum('tgd,cd->tgc', query, all_ck, preferred_element_type=jnp.float32)]
    reduce_sum x3 -> x0, other arithmetic: 11.7 us -> none  [the longest x1 9.75 us: on_device(): jnp.sum(old_w, axis=2, dtype=jnp.float32)]
  transfers between devices with their start and end apart: 6 -> 0, of which waited for: 6 -> 0; matrix products, arithmetic and copies ran while one was open for 6% -> 0% of each run, Pallas kernels for 0% -> 0%
where the time goes in v1:
time: 131 us
  Pallas kernels  128 us (98%)
  local copies, waits for them, and re-layouts  1.67 us (1%)
    pallas_call x1, Pallas kernels, on_device(): pl.pallas_call(kernel, out_shape=jax.ShapeDtypeStruct((ROWS, WIDE), F32),...  128 us

profile of v1, /device:TPU:32, one launch (start us, length us, event | category | flops | bytes accessed | tf_op | source)
XLA Modules:
  0.0 131.2 jit_solution(3658448496902949510)
XLA Ops:
  0.7 0.2 fusion
  0.9 0.7 pad_maximum_fusion
  1.6 128.0 %shard_map.91 = f32[64,1024]{1,0:T(8,128)} custom-call(s32[1]{0:T(128)} %copy.11.start_ref, f32[64,1024]{1,0:T(8,128)} %resid_hbm.1, f32[1,1024]{1,0:T(1,128)} %bitcast.3, bf16[1024,1024]{1,0:T(8,128)(2,1)} %wq_hbm.1, bf16[1024,1024]{1,0:T(8,128)(2,1)} %wk_hbm.1, bf16[1024,1024]{1,0:T(8,128)(2,1)} %wv_hbm.1, bf16[1024,1024]{1,0:T(8,128)(2,1)} %wo_hbm.1, ...), custom_call_target="tpu_custom_call" | custom-call | tf_op jit(solution)/shard_map/pallas_call | solution.py:467
  129.6 1.7 %copy.12 = f32[64,1024]{1,0:T(8,128)} copy(f32[64,1024]{1,0:T(8,128)} %shard_map.91) | data formatting | bytes 524288
  (2 shorter events, 0.0 us)

commit v2 on v1

v2 whole, which is shorter than its diff:
```python
import functools
import math

import jax
import jax.numpy as jnp
from jax import lax
from jax.experimental import pallas as pl
from jax.experimental.pallas import tpu as pltpu
from jax.sharding import PartitionSpec as P

MESH = pl.DeviceIdType.MESH
F32, BF16, I16, I32 = jnp.float32, jnp.bfloat16, jnp.int16, jnp.int32

HD = 128
THETA = 500000.0
ROWS = 64
WIDE = 1024
PROJ = WIDE + 2 * HD
SLOTS = 512
CACHE = 8192
SPAN = 1024
KEYS = CACHE + SPAN
CHUNK = 1024
PART = 32
HALF = 8 * PART
STEP = 8.0
TOP = 32000.0
NEG = -1e30


def rem(a, n):
    return lax.rem(a, jnp.int32(n))


def quantize(dst, v):
    n = v.shape[1]
    fold = jnp.abs(v[:, :HD])
    for k in range(1, n // HD):
        fold = jnp.maximum(fold, jnp.abs(v[:, k * HD : (k + 1) * HD]))
    top = jnp.max(fold, axis=1, keepdims=True)
    e = jnp.ceil(jnp.log2(jnp.maximum(top, 1e-30)) * STEP)
    e = jnp.broadcast_to(e, (v.shape[0], HD))
    up = jnp.exp2(e * (-1.0 / STEP)) * TOP
    for k in range(n // HD):
        dst[:, k * HD : (k + 1) * HD] = jnp.round(v[:, k * HD : (k + 1) * HD] * up).astype(I32).astype(I16)
    dst[:, n : n + HD] = e.astype(I32).astype(I16)


def restore(src, n):
    e = src[:, n : n + HD].astype(I32).astype(F32)
    down = jnp.exp2(e * (1.0 / STEP)) * (1.0 / TOP)
    return jnp.concatenate(
        [src[:, k * HD : (k + 1) * HD].astype(I32).astype(F32) * down for k in range(n // HD)], axis=1
    )


def kernel(
    start_ref, resid_hbm, gain_ref, wq_hbm, wk_hbm, wv_hbm, wo_hbm, ck_hbm, cv_hbm, cos_ref, sin_ref,
    out_ref,
    res, w, wo, g, gs, kv, pb, sq, pp, ks, kr, qs, qr, qh, s_ref, mix, att, op, xs, xr, zs, zr,
    load_sem, w_sem, sq_send, sq_recv, ag_send, ag_recv, gs_send, gs_recv, kv_send, kv_recv,
    ks_send, kr_recv, qs_send, qr_recv, nk_send, nk_recv, at_send, at_recv, xs_send, xr_recv, zs_send, zr_recv,
):
    b = lax.axis_index("blk")
    r = lax.axis_index("red")
    xl, z = lax.div(b, jnp.int32(8)), rem(b, 8)
    xh, y, c = lax.div(r, jnp.int32(8)), rem(lax.div(r, jnp.int32(2)), 4), rem(r, 2)
    chip = lax.div(r, jnp.int32(2))
    head = lax.div(b, jnp.int32(2))
    ox = 1 - xl

    def blk_of(px, pz):
        return px * 8 + rem(pz + 16, 8)

    def red_of(px, py, pc):
        return (px * 4 + rem(py + 8, 4)) * 2 + pc

    z_next = {1: (blk_of(xl, z + 1), r), -1: (blk_of(xl, z - 1), r)}
    x_pair = (blk_of(ox, z), r)
    x_across = (blk_of(ox, z), red_of(1 - xh, y, c))
    sibling = (b, red_of(xh, y, 1 - c))
    others = []
    for dx, dy in ((1, 2), (0, 1), (1, 0), (0, 3), (1, 1), (0, 2), (1, 3)):
        p = lax.div(red_of(rem(xh + dx, 2), y + dy, 0), jnp.int32(2))
        others.append((p, (b, p * 2 + c)))

    barrier = pltpu.get_barrier_semaphore()
    peers = [(b, rem(r + i, 16)) for i in range(1, 16)] + [z_next[1], z_next[-1], x_pair, x_across]
    for p in peers:
        pl.semaphore_signal(barrier, inc=1, device_id=p, device_id_type=MESH)

    mine = pl.ds(pl.multiple_of(r * SLOTS, SLOTS), SLOTS)
    my_cols = pl.ds(pl.multiple_of(head * HD, HD), HD)
    pair_head = lax.div(blk_of(ox, z), jnp.int32(2))
    pair_cols = pl.ds(pl.multiple_of(pair_head * HD, HD), HD)
    loads = [
        pltpu.make_async_copy(resid_hbm, res, load_sem.at[0]),
        pltpu.make_async_copy(ck_hbm.at[:, my_cols], kv.at[mine, 0:HD], load_sem.at[1]),
        pltpu.make_async_copy(cv_hbm.at[:, my_cols], kv.at[mine, HD : 2 * HD], load_sem.at[2]),
        pltpu.make_async_copy(ck_hbm.at[:, pair_cols], pb.at[:, 0:HD], load_sem.at[3]),
        pltpu.make_async_copy(cv_hbm.at[:, pair_cols], pb.at[:, HD : 2 * HD], load_sem.at[4]),
        pltpu.make_async_copy(wq_hbm, w.at[0, :, 0:WIDE], load_sem.at[5]),
        pltpu.make_async_copy(wk_hbm.at[:, my_cols], w.at[0, :, WIDE : WIDE + HD], load_sem.at[6]),
        pltpu.make_async_copy(wv_hbm.at[:, my_cols], w.at[0, :, WIDE + HD : PROJ], load_sem.at[7]),
        pltpu.make_async_copy(wo_hbm, wo, load_sem.at[8]),
    ]
    for cp in loads:
        cp.start()

    sends = []

    def send(src, dst, ssem, rsem, to):
        cp = pltpu.make_async_remote_copy(
            src_ref=src, dst_ref=dst, send_sem=ssem, recv_sem=rsem, device_id=to, device_id_type=MESH
        )
        cp.start()
        sends.append(cp)

    def arrived(dst, rsem):
        pltpu.make_async_remote_copy(
            src_ref=dst, dst_ref=dst, send_sem=load_sem.at[0], recv_sem=rsem, device_id=sibling, device_id_type=MESH
        ).wait_recv()

    loads[0].wait()
    fold = jnp.zeros((ROWS, HD), F32)
    for k in range(WIDE // HD):
        v = res[:, k * HD : (k + 1) * HD]
        fold = fold + v * v
    square = jnp.concatenate([fold, jnp.zeros((HD - ROWS, HD), F32)], axis=0).T
    sq[r] = jnp.broadcast_to(jnp.sum(square, axis=0, keepdims=True), (8, HD))
    pl.semaphore_wait(barrier, len(peers))
    for i, (p, to) in enumerate(others):
        send(sq.at[r], sq.at[r], sq_send.at[2 * i], sq_recv.at[r], to)
        send(sq.at[r], sq.at[r], sq_send.at[2 * i + 1], sq_recv.at[r], (b, p * 2 + 1 - c))
    send(sq.at[r], sq.at[r], sq_send.at[14], sq_recv.at[r], sibling)

    for cp in loads[1:5]:
        cp.wait()

    def kv_rows(red):
        return kv.at[pl.ds(pl.multiple_of(red * SLOTS, SLOTS), SLOTS), 0 : 2 * HD]

    kv_count = [0]

    def kv_send_to(red, to, src=None):
        send(kv_rows(red) if src is None else src, kv_rows(red), kv_send.at[kv_count[0]], kv_recv.at[red], to)
        kv_count[0] += 1

    kv_send_to(r, x_across, src=pb)
    for d in (1, 3, 2):
        kv_send_to(r, (b, red_of(xh, y + d, c)))

    kv[:, 2 * HD : 3 * HD] = jnp.ones((KEYS, HD), BF16)

    for i in range(1, 16):
        p = rem(r + i, 16)
        arrived(sq.at[p], sq_recv.at[p])
    total = jnp.sum(sq[...], axis=0)[0:1]
    column = jnp.broadcast_to(total, (HD, HD)).T[:ROWS]
    factor = lax.rsqrt(column / (WIDE * 16.0) + 1e-05)
    gain = gain_ref[...]

    def g_at(h, px, pz):
        pz = rem(pz + 16, 8)
        return g.at[h, rem(pz, 2), px * 4 + lax.div(pz, jnp.int32(2))]

    ag_count = [0, 0]

    def g_wait(h, px, d):
        pz = z + (1 - 2 * h) * d
        arrived(g_at(h, px, pz), ag_recv.at[h, blk_of(px, pz)])

    def g_send(h, px, d, *to):
        pz = z + (1 - 2 * h) * d
        for t in to:
            device = x_pair if t == 0 else z_next[t * (1 - 2 * h)]
            send(g_at(h, px, pz), g_at(h, px, pz), ag_send.at[h, ag_count[h]], ag_recv.at[h, blk_of(px, pz)], device)
            ag_count[h] += 1

    gs_count = [0, 0]

    def g_trade(h, px, d, e):
        s = 1 - 2 * h
        pz = rem(z + 16 + jnp.where(rem(z + 16 + s * d, 2) == 1 - c, s * d, s * e), 8)
        j = px * 4 + lax.div(pz, jnp.int32(2))
        send(g.at[h, 1 - c, j], gs.at[h, j], gs_send.at[h, gs_count[h]], gs_recv.at[h, j], sibling)
        gs_count[h] += 1

    def gather(h, stage):
        if stage == 0:
            rows = slice(h * PART, (h + 1) * PART)
            slot = g_at(h, xl, z)
            for k in range(WIDE // HD):
                lanes = slice(k * HD, (k + 1) * HD)
                slot[:, lanes] = (res[rows, lanes] * factor[rows] * gain[:, lanes]).astype(BF16)
            g_send(h, xl, 0, 1, -1, 0)
        if stage == 1:
            g_wait(h, xl, -1)
            g_send(h, xl, -1, 1)
            g_wait(h, xl, 1)
            g_send(h, xl, 1, -1)
            g_wait(h, ox, 0)
            g_send(h, ox, 0, 1, -1)
            g_trade(h, xl, 0, -1)
        if stage == 2:
            g_wait(h, xl, -2)
            g_send(h, xl, -2, 1)
            g_wait(h, xl, 2)
            g_send(h, xl, 2, -1)
            g_wait(h, ox, -1)
            g_send(h, ox, -1, 1)
            g_wait(h, ox, 1)
            g_send(h, ox, 1, -1)
            g_trade(h, xl, 1, -2)
            g_trade(h, ox, 0, -1)
        if stage == 3:
            g_wait(h, xl, -3)
            g_send(h, xl, -3, 1, 0)
            g_wait(h, xl, 3)
            g_send(h, xl, 3, 0)
            g_trade(h, xl, 2, -3)
        if stage == 4:
            g_wait(h, xl, -4)
            g_send(h, xl, -4, 0)
            g_trade(h, xl, 3, -4)
        if stage == 5:
            g_wait(h, ox, -2)
            g_wait(h, ox, 2)
            g_trade(h, ox, 1, -2)
            g_wait(h, ox, -3)
            g_wait(h, ox, 3)
            g_trade(h, ox, 2, -3)
        if stage == 6:
            g_wait(h, ox, -4)
            g_trade(h, ox, 3, -4)
            for j in range(8):
                arrived(gs.at[h, j], gs_recv.at[h, j])

    def project(h):
        x0 = g.at[h, c][...].reshape(8 * PART, WIDE)
        x1 = gs[h].reshape(8 * PART, WIDE)

        def columns(n):
            lanes = slice(n * 256, (n + 1) * 256)
            t = jnp.dot(x0, w[0, :, lanes], preferred_element_type=F32)
            t = t + jnp.dot(x1, w[1, :, lanes], preferred_element_type=F32)
            pp[h, :, :, lanes] = t.reshape(8, PART, 256)

        columns(WIDE // 256)
        for i, (p, to) in enumerate(others):
            quantize(ks.at[h, i], pp[h, p, :, WIDE:PROJ])
            send(ks.at[h, i], kr.at[h, chip], ks_send.at[h, i], kr_recv.at[h, chip], to)
        for n in range(WIDE // 256):
            columns(n)
        for i, (p, to) in enumerate(others):
            quantize(qs.at[h, i], pp[h, p, :, 0:WIDE])
            send(qs.at[h, i], qr.at[h, chip], qs_send.at[h, i], qr_recv.at[h, chip], to)

    gather(0, 0)
    gather(1, 0)
    send(kv_rows(r), kv_rows(r), kv_send.at[kv_count[0]], kv_recv.at[r], sibling)
    kv_count[0] += 1
    for cp in loads[5:8]:
        cp.wait()
    send(w.at[0], w.at[1], w_sem.at[0], w_sem.at[1], sibling)
    gather(0, 1)
    gather(1, 1)
    r_across = red_of(1 - xh, y, c)
    arrived(kv_rows(r_across), kv_recv.at[r_across])
    for d in (1, 3, 2):
        kv_send_to(r_across, (b, red_of(xh, y + d, c)))
    gather(0, 2)
    gather(1, 2)
    kv_send_to(r_across, sibling)
    gather(0, 3)
    gather(1, 3)
    gather(0, 4)
    gather(0, 5)
    gather(1, 4)
    gather(0, 6)
    arrived(w.at[1], w_sem.at[1])
    project(0)
    gather(1, 5)
    gather(1, 6)
    project(1)

    for red in (
        red_of(xh, y + 1, c), red_of(xh, y + 3, c), red_of(xh, y + 2, c),
        red_of(1 - xh, y + 1, c), red_of(1 - xh, y + 3, c), red_of(1 - xh, y + 2, c),
    ):
        arrived(kv_rows(red), kv_recv.at[red])
        kv_send_to(red, sibling)

    def turn(h, v):
        rows = slice(h * PART, (h + 1) * PART)
        return (v * cos_ref[rows] + pltpu.roll(v, HD // 2, 1) * sin_ref[rows]).astype(BF16)

    for h in range(2):
        new = pp[h, chip, :, WIDE:PROJ]
        for p, _ in others:
            arrived(kr.at[h, p], kr_recv.at[h, p])
            new = new + restore(kr.at[h, p], 2 * HD)
        fresh = pl.ds(pl.multiple_of(CACHE + r * ROWS + h * PART, PART), PART)
        kv[fresh, 0:HD] = turn(h, new[:, 0:HD])
        kv[fresh, HD : 2 * HD] = new[:, HD : 2 * HD].astype(BF16)

    def nk_rows(red):
        return kv.at[pl.ds(pl.multiple_of(CACHE + red * ROWS, ROWS), ROWS), 0 : 2 * HD]

    def nk_to(slot, red, to):
        send(nk_rows(red), nk_rows(red), nk_send.at[slot], nk_recv.at[red], to)

    for i, (p, to) in enumerate(others):
        nk_to(i, r, to)
    nk_to(7, r, sibling)

    for k in range(8):
        red = rem(chip + k, 8) * 2 + 1 - c
        arrived(kv_rows(red), kv_recv.at[red])
    start = start_ref[0]
    turn_log = HD ** (-0.5) * math.log2(math.e)

    def scores(h, n):
        keys = kv[pl.ds(pl.multiple_of(n * CHUNK, CHUNK), CHUNK), 0:HD]
        return lax.dot_general(qh[h], keys, (((1,), (1,)), ((), ())), preferred_element_type=F32)

    def keep(h, n, t, top):
        s_ref[h, :, pl.ds(pl.multiple_of(n * CHUNK, CHUNK), CHUNK)] = t
        for k in range(CHUNK // HD):
            top = jnp.maximum(top, t[:, k * HD : (k + 1) * HD])
        return top

    tops = []
    for h in range(2):
        query = pp[h, chip, :, 0:WIDE]
        for p, _ in others:
            arrived(qr.at[h, p], qr_recv.at[h, p])
            query = query + restore(qr.at[h, p], WIDE)
        for k in range(8):
            qh[h, k * PART : (k + 1) * PART, :] = turn(h, query[:, k * HD : (k + 1) * HD])

        def plain(n, top, h=h):
            return keep(h, n, scores(h, n), top)

        def partly(n, top, h=h):
            slot = n * CHUNK + lax.broadcasted_iota(I32, (1, CHUNK), 1)
            return keep(h, n, scores(h, n) + jnp.where(slot < start, 0.0, NEG), top)

        top = jnp.full((HALF, HD), NEG, F32)
        top = lax.fori_loop(0, 4, plain, top)
        tops.append(lax.fori_loop(4, 8, partly, top))

    for i, (p, _) in enumerate(others):
        red = p * 2 + c
        arrived(nk_rows(red), nk_recv.at[red])
        nk_to(8 + i, red, sibling)
    for k in range(8):
        red = rem(chip + k, 8) * 2 + 1 - c
        arrived(nk_rows(red), nk_recv.at[red])

    at_count = [0, 0]

    def at_to(h, red, to):
        send(att.at[h, red], att.at[h, red], at_send.at[h, at_count[h]], at_recv.at[h, red], to)
        at_count[h] += 1

    for h in range(2):
        token = r * ROWS + h * PART + rem(lax.broadcasted_iota(I32, (HALF, CHUNK), 0), PART)
        ahead = lax.broadcasted_iota(I32, (HALF, CHUNK), 1) > token
        top = keep(h, 8, jnp.where(ahead, NEG, scores(h, 8)), tops[h])
        peak = jnp.broadcast_to(jnp.max(top, axis=1, keepdims=True), (HALF, HD))

        mix[...] = jnp.zeros_like(mix)

        def weigh(n, _, h=h, peak=peak):
            base = n * CHUNK
            parts = []
            for k in range(CHUNK // HD):
                t = s_ref[h, :, pl.ds(pl.multiple_of(base + k * HD, HD), HD)]
                parts.append(jnp.exp2((t - peak) * turn_log).astype(BF16))
            wts = jnp.concatenate(parts, axis=1)
            vals = kv[pl.ds(pl.multiple_of(base, CHUNK), CHUNK), HD : 3 * HD]
            mix[...] += jnp.dot(wts, vals, preferred_element_type=F32)
            return 0

        lax.fori_loop(0, 9, weigh, 0)
        done = (mix[:, 0:HD] / mix[:, HD : 2 * HD]).astype(BF16)
        for k in range(8):
            att[h, r, :, k * HD : (k + 1) * HD] = done[k * PART : (k + 1) * PART, :]
        for p, to in others:
            at_to(h, r, to)
        at_to(h, r, sibling)

    loads[8].wait()

    def project_out(h):
        for p, _ in others:
            red = p * 2 + c
            arrived(att.at[h, red], at_recv.at[h, red])
            at_to(h, red, sibling)
        for k in range(8):
            red = rem(chip + k, 8) * 2 + 1 - c
            arrived(att.at[h, red], at_recv.at[h, red])
        for m in range(2):
            x = att[h, m * 8 : (m + 1) * 8].reshape(8 * PART, WIDE)
            for n in range(WIDE // 256):
                lanes = slice(n * 256, (n + 1) * 256)
                t = jnp.dot(x, wo[:, lanes], preferred_element_type=F32)
                op[h, m * 8 : (m + 1) * 8, :, lanes] = t.reshape(8, PART, 256)

    def ring(h, stage):
        s = 1 - 2 * h
        up, down = z_next[s], z_next[-s]

        def own(d):
            return op[h, blk_of(xl, z + s * d)]

        def other(d):
            return op[h, blk_of(ox, z + s * d)]

        def x_send(k, v):
            quantize(xs.at[h, k], v)
            send(xs.at[h, k], xr.at[h, k], xs_send.at[h, k], xr_recv.at[h, k], x_pair)

        def x_get(k):
            arrived(xr.at[h, k], xr_recv.at[h, k])
            return restore(xr.at[h, k], WIDE)

        def z_send(k, v, to):
            quantize(zs.at[h, k], v)
            send(zs.at[h, k], zr.at[h, k], zs_send.at[h, k], zr_recv.at[h, k], to)

        def z_get(k):
            arrived(zr.at[h, k], zr_recv.at[h, k])
            return restore(zr.at[h, k], WIDE)

        if stage == 0:
            x_send(0, other(4))
            z_send(4, other(2), up)
            z_send(9, other(-2), down)
            x_send(1, other(-3))
            x_send(2, other(3))
        if stage == 1:
            z_send(0, own(4) + x_get(0), up)
            z_send(6, own(-3) + x_get(1), down)
        if stage == 2:
            z_send(5, other(1) + z_get(4), up)
            z_send(10, other(-1) + z_get(9), down)
        if stage == 3:
            z_send(1, own(3) + z_get(0) + x_get(2), up)
            z_send(7, own(-2) + z_get(6), down)
        if stage == 4:
            x_send(3, other(0) + z_get(5) + z_get(10))
        if stage == 5:
            z_send(2, own(2) + z_get(1), up)
            z_send(8, own(-1) + z_get(7), down)
        if stage == 6:
            z_send(3, own(1) + z_get(2), up)
        if stage == 7:
            rows = slice(h * PART, (h + 1) * PART)
            out_ref[rows] = res[rows] + (own(0) + x_get(3) + z_get(8) + z_get(3))

    project_out(0)
    ring(0, 0)
    ring(0, 1)
    ring(0, 2)
    project_out(1)
    ring(1, 0)
    ring(0, 3)
    ring(1, 1)
    ring(1, 2)
    ring(0, 4)
    ring(0, 5)
    ring(1, 3)
    ring(0, 6)
    ring(1, 4)
    ring(1, 5)
    ring(0, 7)
    ring(1, 6)
    ring(1, 7)

    for cp in sends:
        cp.wait_send()


def on_device(resid, norm_gain, w_query, w_key, w_value, w_out, cache_key, cache_value, prefix_len):
    r = lax.axis_index("red")
    half = HD // 2
    steps = jnp.arange(half, dtype=F32)
    freq = THETA ** (-(steps * 2.0) / HD)
    positions = prefix_len[0] + r * ROWS + jnp.arange(ROWS, dtype=I32)
    angle = positions.astype(F32)[:, None] * freq[None, :]
    cosine, sine = jnp.cos(angle), jnp.sin(angle)
    cosine = jnp.concatenate([cosine, cosine], axis=1)
    sine = jnp.concatenate([-sine, sine], axis=1)
    vmem = pl.BlockSpec(memory_space=pltpu.VMEM)
    hbm = pl.BlockSpec(memory_space=pl.ANY)
    dma = pltpu.SemaphoreType.DMA
    scratch = [
        pltpu.VMEM((ROWS, WIDE), F32),
        pltpu.VMEM((2, WIDE, PROJ), BF16),
        pltpu.VMEM((WIDE, WIDE), BF16),
        pltpu.VMEM((2, 2, 8, PART, WIDE), BF16),
        pltpu.VMEM((2, 8, PART, WIDE), BF16),
        pltpu.VMEM((KEYS, 3 * HD), BF16),
        pltpu.VMEM((SLOTS, 2 * HD), BF16),
        pltpu.VMEM((16, 8, HD), F32),
        pltpu.VMEM((2, 8, PART, PROJ), F32),
        pltpu.VMEM((2, 7, PART, 3 * HD), I16),
        pltpu.VMEM((2, 8, PART, 3 * HD), I16),
        pltpu.VMEM((2, 7, PART, WIDE + HD), I16),
        pltpu.VMEM((2, 8, PART, WIDE + HD), I16),
        pltpu.VMEM((2, 8 * PART, HD), BF16),
        pltpu.VMEM((2, HALF, KEYS), F32),
        pltpu.VMEM((HALF, 2 * HD), F32),
        pltpu.VMEM((2, 16, PART, WIDE), BF16),
        pltpu.VMEM((2, 16, PART, WIDE), F32),
        pltpu.VMEM((2, 4, PART, WIDE + HD), I16),
        pltpu.VMEM((2, 4, PART, WIDE + HD), I16),
        pltpu.VMEM((2, 11, PART, WIDE + HD), I16),
        pltpu.VMEM((2, 11, PART, WIDE + HD), I16),
        dma((9,)), dma((2,)), dma((15,)), dma((16,)),
        dma((2, 15)), dma((2, 16)), dma((2, 8)), dma((2, 8)),
        dma((15,)), dma((16,)),
        dma((2, 7)), dma((2, 8)), dma((2, 7)), dma((2, 8)),
        dma((15,)), dma((16,)),
        dma((2, 15)), dma((2, 16)),
        dma((2, 4)), dma((2, 4)), dma((2, 11)), dma((2, 11)),
    ]
    return pl.pallas_call(
        kernel,
        out_shape=jax.ShapeDtypeStruct((ROWS, WIDE), F32),
        in_specs=[pl.BlockSpec(memory_space=pltpu.SMEM), hbm, vmem, hbm, hbm, hbm, hbm, hbm, hbm, vmem, vmem],
        out_specs=vmem,
        scratch_shapes=scratch,
        compiler_params=pltpu.CompilerParams(
            collective_id=0, has_side_effects=True, vmem_limit_bytes=58 * 1024 * 1024
        ),
    )(prefix_len, resid, norm_gain[None, :], w_query, w_key, w_value, w_out, cache_key, cache_value, cosine, sine)


def solution(mesh):
    placed = (
        P("blk", "red"), P("red"), P("red", "blk"), P("red", None), P("red", None), P("blk", "red"),
        P("red", None), P("red", None), P(),
    )
    return jax.shard_map(on_device, mesh=mesh, in_specs=placed, out_specs=P("blk", "red"), check_vma=False)
```

time: 131 us -> 114 us (0.87)
  Pallas kernels: 128 us -> 110 us
    pallas_call x1, Pallas kernels: 128 us -> 110 us  [on_device(): pl.pallas_call(kernel, out_shape=jax.ShapeDtypeStruct((ROWS, WIDE), F32),...]
where the time goes in v2:
time: 114 us; the launch traced here: 113 us
  Pallas kernels  110 us (96%)
  local copies, waits for them, and re-layouts  1.67 us (1%)
    pallas_call x1, Pallas kernels, on_device(): pl.pallas_call(kernel, out_shape=jax.ShapeDtypeStruct((ROWS, WIDE), F32),...  110 us

profile of v2, /device:TPU:32, one launch (start us, length us, event | category | flops | bytes accessed | tf_op | source)
XLA Modules:
  0.0 113.2 jit_solution(9523922364916955768)
XLA Ops:
  0.7 0.2 fusion
  0.9 0.7 pad_maximum_fusion
  1.6 109.9 %shard_map.91 = f32[64,1024]{1,0:T(8,128)} custom-call(s32[1]{0:T(128)} %copy.11.start_ref, f32[64,1024]{1,0:T(8,128)} %resid_hbm.1, f32[1,1024]{1,0:T(1,128)} %bitcast.3, bf16[1024,1024]{1,0:T(8,128)(2,1)} %wq_hbm.1, bf16[1024,1024]{1,0:T(8,128)(2,1)} %wk_hbm.1, bf16[1024,1024]{1,0:T(8,128)(2,1)} %wv_hbm.1, bf16[1024,1024]{1,0:T(8,128)(2,1)} %wo_hbm.1, ...), custom_call_target="tpu_custom_call" | custom-call | tf_op jit(solution)/shard_map/pallas_call | solution.py:530
  111.5 1.7 %copy.12 = f32[64,1024]{1,0:T(8,128)} copy(f32[64,1024]{1,0:T(8,128)} %shard_map.91) | data formatting | bytes 524288
  (2 shorter events, 0.0 us)

commit v3 on v2

v3 whole, which is shorter than its diff:
```python
import functools
import math

import jax
import jax.numpy as jnp
from jax import lax
from jax.experimental import pallas as pl
from jax.experimental.pallas import tpu as pltpu
from jax.sharding import PartitionSpec as P

MESH = pl.DeviceIdType.MESH
F32, BF16, I16, I32 = jnp.float32, jnp.bfloat16, jnp.int16, jnp.int32

HD = 128
THETA = 500000.0
ROWS = 64
WIDE = 1024
PROJ = WIDE + 2 * HD
SLOTS = 512
CACHE = 8192
SPAN = 1024
KEYS = CACHE + SPAN
CHUNK = 1024
PIECES = ((0, 32), (32, 32))
EARLY = 4
LANES = 32
STEP = 8.0
TOP = 32000.0
NEG = -1e30


def rem(a, n):
    return lax.rem(a, jnp.int32(n))


def tiles(rows, lanes):
    return rows // 16 * (lanes // HD) + 1


def quantize(dst, v):
    wide, groups = v.shape[1] // HD, v.shape[0] // 16
    lane = lax.broadcasted_iota(I32, (16, HD), 1)
    exponents = jnp.zeros((16, HD), F32)
    for m in range(groups):
        rows = v[m * 16 : (m + 1) * 16]
        fold = jnp.abs(rows[:, :HD])
        for k in range(1, wide):
            fold = jnp.maximum(fold, jnp.abs(rows[:, k * HD : (k + 1) * HD]))
        top = jnp.max(fold, axis=1, keepdims=True)
        e = jnp.broadcast_to(jnp.ceil(jnp.log2(jnp.maximum(top, 1e-30)) * STEP), (16, HD))
        exponents = e if m == 0 else jnp.where(lane < m * LANES, exponents, e)
        up = jnp.exp2(e * (-1.0 / STEP)) * TOP
        for k in range(wide):
            dst[m * wide + k] = jnp.round(rows[:, k * HD : (k + 1) * HD] * up).astype(I32).astype(I16)
    dst[groups * wide] = exponents.astype(I32).astype(I16)


def restore(src, groups, wide):
    e = src[groups * wide].astype(I32).astype(F32)
    parts = []
    for m in range(groups):
        lane = m * LANES
        down = jnp.broadcast_to(jnp.exp2(e[:, lane : lane + 1] * (1.0 / STEP)) * (1.0 / TOP), (16, HD))
        parts.append(
            jnp.concatenate([src[m * wide + k].astype(I32).astype(F32) * down for k in range(wide)], axis=1)
        )
    return jnp.concatenate(parts, axis=0)


def kernel(
    start_ref, resid_hbm, gain_ref, wq_hbm, wk_hbm, wv_hbm, wo_hbm, ck_hbm, cv_hbm, freq_ref,
    out_ref,
    cos_ref, sin_ref, res, w, wo, kv, pb, sq,
    load_sem, w_sem, sq_send, sq_recv, kv_send, kv_recv, nk_send, nk_recv,
    *per_piece,
):
    (
        g, gs, pp, ks, kr, qs, qr, qh, s_ref, mix,
        att, op, xs, xr, zs, zr,
        ag_send, ag_recv, gs_send, gs_recv, ks_send, kr_recv, qs_send, qr_recv,
        at_send, at_recv, xs_send, xr_recv, zs_send, zr_recv,
    ) = [per_piece[k :: 30] for k in range(30)]
    count = len(PIECES)
    sense = [1 - 2 * (h % 2) for h in range(count)]
    extent = [slice(first, first + rows) for first, rows in PIECES]
    size = [rows for _, rows in PIECES]
    b = lax.axis_index("blk")
    r = lax.axis_index("red")
    xl, z = lax.div(b, jnp.int32(8)), rem(b, 8)
    xh, y, c = lax.div(r, jnp.int32(8)), rem(lax.div(r, jnp.int32(2)), 4), rem(r, 2)
    chip = lax.div(r, jnp.int32(2))
    head = lax.div(b, jnp.int32(2))
    ox = 1 - xl

    def blk_of(px, pz):
        return px * 8 + rem(pz + 16, 8)

    def red_of(px, py, pc):
        return (px * 4 + rem(py + 8, 4)) * 2 + pc

    z_next = {1: (blk_of(xl, z + 1), r), -1: (blk_of(xl, z - 1), r)}
    z_over = {1: (blk_of(xl, z + 2), r), -1: (blk_of(xl, z - 2), r)}
    x_pair = (blk_of(ox, z), r)
    x_across = (blk_of(ox, z), red_of(1 - xh, y, c))
    sibling = (b, red_of(xh, y, 1 - c))
    others = []
    for dx, dy in ((1, 2), (0, 1), (1, 0), (0, 3), (1, 1), (0, 2), (1, 3)):
        p = lax.div(red_of(rem(xh + dx, 2), y + dy, 0), jnp.int32(2))
        others.append((p, (b, p * 2 + c)))

    nearest = [others[i] for i in (1, 3, 2, 5, 4, 6, 0)]

    barrier = pltpu.get_barrier_semaphore()
    peers = [(b, rem(r + i, 16)) for i in range(1, 16)] + [z_next[1], z_next[-1], z_over[1], z_over[-1], x_pair, x_across]
    for p in peers:
        pl.semaphore_signal(barrier, inc=1, device_id=p, device_id_type=MESH)

    mine = pl.ds(pl.multiple_of(r * SLOTS, SLOTS), SLOTS)
    my_cols = pl.ds(pl.multiple_of(head * HD, HD), HD)
    pair_head = lax.div(blk_of(ox, z), jnp.int32(2))
    pair_cols = pl.ds(pl.multiple_of(pair_head * HD, HD), HD)
    loads = [
        pltpu.make_async_copy(resid_hbm, res, load_sem.at[0]),
        pltpu.make_async_copy(ck_hbm.at[:, my_cols], kv.at[mine, 0:HD], load_sem.at[1]),
        pltpu.make_async_copy(cv_hbm.at[:, my_cols], kv.at[mine, HD : 2 * HD], load_sem.at[2]),
        pltpu.make_async_copy(ck_hbm.at[:, pair_cols], pb.at[:, 0:HD], load_sem.at[3]),
        pltpu.make_async_copy(cv_hbm.at[:, pair_cols], pb.at[:, HD : 2 * HD], load_sem.at[4]),
        pltpu.make_async_copy(wq_hbm, w.at[0, :, 0:WIDE], load_sem.at[5]),
        pltpu.make_async_copy(wk_hbm.at[:, my_cols], w.at[0, :, WIDE : WIDE + HD], load_sem.at[6]),
        pltpu.make_async_copy(wv_hbm.at[:, my_cols], w.at[0, :, WIDE + HD : PROJ], load_sem.at[7]),
        pltpu.make_async_copy(wo_hbm, wo, load_sem.at[8]),
    ]
    for cp in loads:
        cp.start()

    sends = []

    def send(src, dst, ssem, rsem, to):
        cp = pltpu.make_async_remote_copy(
            src_ref=src, dst_ref=dst, send_sem=ssem, recv_sem=rsem, device_id=to, device_id_type=MESH
        )
        cp.start()
        sends.append(cp)

    def sent(keep):
        for cp in sends[: len(sends) - len(keep)]:
            cp.wait_send()
        sends[:] = list(keep)

    def arrived(dst, rsem):
        pltpu.make_async_remote_copy(
            src_ref=dst, dst_ref=dst, send_sem=load_sem.at[0], recv_sem=rsem, device_id=sibling, device_id_type=MESH
        ).wait_recv()

    kv[:, 2 * HD : 3 * HD] = jnp.ones((KEYS, HD), BF16)

    start = start_ref[0]
    position = (start + r * ROWS + lax.broadcasted_iota(I32, (ROWS, HD), 0)).astype(F32)
    angle = position * freq_ref[...]
    first = lax.broadcasted_iota(I32, (ROWS, HD), 1) < HD // 2
    cos_ref[...] = jnp.cos(angle)
    sine = jnp.sin(angle)
    sin_ref[...] = jnp.where(first, -sine, sine)

    loads[0].wait()
    fold = jnp.zeros((ROWS, HD), F32)
    for k in range(WIDE // HD):
        v = res[:, k * HD : (k + 1) * HD]
        fold = fold + v * v
    square = jnp.concatenate([fold, jnp.zeros((HD - ROWS, HD), F32)], axis=0).T
    sq[r] = jnp.broadcast_to(jnp.sum(square, axis=0, keepdims=True), (8, HD))
    pl.semaphore_wait(barrier, len(peers))
    for i, (p, to) in enumerate(others):
        send(sq.at[r], sq.at[r], sq_send.at[2 * i], sq_recv.at[r], to)
        send(sq.at[r], sq.at[r], sq_send.at[2 * i + 1], sq_recv.at[r], (b, p * 2 + 1 - c))
    send(sq.at[r], sq.at[r], sq_send.at[14], sq_recv.at[r], sibling)

    for cp in loads[1:5]:
        cp.wait()

    def kv_rows(red):
        return kv.at[pl.ds(pl.multiple_of(red * SLOTS, SLOTS), SLOTS), 0 : 2 * HD]

    kv_count = [0]

    def kv_send_to(red, to, src=None):
        send(kv_rows(red) if src is None else src, kv_rows(red), kv_send.at[kv_count[0]], kv_recv.at[red], to)
        kv_count[0] += 1

    kv_send_to(r, x_across, src=pb)
    for d in (1, 3, 2):
        kv_send_to(r, (b, red_of(xh, y + d, c)))

    for i in range(1, 16):
        p = rem(r + i, 16)
        arrived(sq.at[p], sq_recv.at[p])
    total = jnp.sum(sq[...], axis=0)[0:1]
    column = jnp.broadcast_to(total, (HD, HD)).T[:ROWS]
    factor = lax.rsqrt(column / (WIDE * 16.0) + 1e-05)
    gain = gain_ref[...]

    def g_at(h, px, pz):
        pz = rem(pz + 16, 8)
        return g[h].at[rem(pz, 2), px * 4 + lax.div(pz, jnp.int32(2))]

    ag_count = [0] * count

    def g_wait(h, px, d):
        pz = z + sense[h] * d
        arrived(g_at(h, px, pz), ag_recv[h].at[blk_of(px, pz)])

    def g_send(h, px, d, *to):
        pz = z + sense[h] * d
        for t in to:
            s = sense[h] * t
            device = {0: x_pair, 1: z_next.get(s), 2: z_over.get(s // 2)}[abs(t)]
            send(g_at(h, px, pz), g_at(h, px, pz), ag_send[h].at[ag_count[h]], ag_recv[h].at[blk_of(px, pz)], device)
            ag_count[h] += 1

    gs_count = [0] * count

    def g_trade(h, px, d, e):
        s = sense[h]
        pz = rem(z + 16 + jnp.where(rem(z + 16 + s * d, 2) == 1 - c, s * d, s * e), 8)
        j = px * 4 + lax.div(pz, jnp.int32(2))
        send(g[h].at[1 - c, j], gs[h].at[j], gs_send[h].at[gs_count[h]], gs_recv[h].at[j], sibling)
        gs_count[h] += 1

    def gather(h, stage):
        if stage == 0:
            rows = extent[h]
            slot = g_at(h, xl, z)
            for k in range(WIDE // HD):
                lanes = slice(k * HD, (k + 1) * HD)
                slot[:, lanes] = (res[rows, lanes] * factor[rows] * gain[:, lanes]).astype(BF16)
            g_send(h, xl, 0, 1, -1, 0)
        if stage == 1:
            g_wait(h, xl, -1)
            g_send(h, xl, -1, 1)
            g_wait(h, xl, 1)
            g_send(h, xl, 1, -1)
            g_wait(h, ox, 0)
            g_send(h, ox, 0, 1, -1)
            g_trade(h, xl, 0, -1)
        if stage == 2:
            g_wait(h, xl, -2)
            g_send(h, xl, -2, 1)
            g_wait(h, xl, 2)
            g_send(h, xl, 2, -1)
            g_wait(h, ox, -1)
            g_send(h, ox, -1, 1)
            g_wait(h, ox, 1)
            g_send(h, ox, 1, -1)
            g_trade(h, xl, 1, -2)
            g_trade(h, ox, 0, -1)
        if stage == 3:
            g_wait(h, xl, -3)
            g_send(h, xl, -3, 1, 0)
            g_wait(h, xl, 3)
            g_send(h, xl, 3, 0)
            g_trade(h, xl, 2, -3)
        if stage == 4:
            g_wait(h, xl, -4)
            g_send(h, xl, -4, 0)
            g_trade(h, xl, 3, -4)
        if stage == 5:
            g_wait(h, ox, -2)
            g_wait(h, ox, 2)
            g_trade(h, ox, 1, -2)
            g_wait(h, ox, -3)
            g_wait(h, ox, 3)
            g_trade(h, ox, 2, -3)
        if stage == 6:
            g_wait(h, ox, -4)
            g_trade(h, ox, 3, -4)
            for j in range(8):
                arrived(gs[h].at[j], gs_recv[h].at[j])

    def project(h):
        x0 = g[h].at[c][...].reshape(8 * size[h], WIDE)
        x1 = gs[h][...].reshape(8 * size[h], WIDE)

        def columns(n):
            lanes = slice(n * 256, (n + 1) * 256)
            t = jnp.dot(x0, w[0, :, lanes], preferred_element_type=F32)
            t = t + jnp.dot(x1, w[1, :, lanes], preferred_element_type=F32)
            pp[h][:, :, lanes] = t.reshape(8, size[h], 256)

        columns(WIDE // 256)
        for i, (p, to) in enumerate(others):
            quantize(ks[h].at[i], pp[h][p, :, WIDE:PROJ])
            send(ks[h].at[i], kr[h].at[chip], ks_send[h].at[i], kr_recv[h].at[chip], to)
        for n in range(WIDE // 256):
            columns(n)

    def send_queries(h, which):
        for i in which:
            p, to = others[i]
            quantize(qs[h].at[i], pp[h][p, :, 0:WIDE])
            send(qs[h].at[i], qr[h].at[chip], qs_send[h].at[i], qr_recv[h].at[chip], to)

    for h in range(count):
        gather(h, 0)
    send(kv_rows(r), kv_rows(r), kv_send.at[kv_count[0]], kv_recv.at[r], sibling)
    kv_count[0] += 1
    for cp in loads[5:8]:
        cp.wait()
    send(w.at[0], w.at[1], w_sem.at[0], w_sem.at[1], sibling)
    for h in range(count):
        gather(h, 1)
    r_across = red_of(1 - xh, y, c)
    arrived(kv_rows(r_across), kv_recv.at[r_across])
    for d in (1, 3, 2):
        kv_send_to(r_across, (b, red_of(xh, y + d, c)))
    for h in range(count):
        gather(h, 2)
    kv_send_to(r_across, sibling)
    for h in range(count):
        gather(h, 3)
    gather(0, 4)
    for h in range(count):
        gather(h, 5)
        if h + 1 < count:
            gather(h + 1, 4)
        gather(h, 6)
        if h == 0:
            arrived(w.at[1], w_sem.at[1])
        project(h)
        send_queries(h, range(7 if h + 1 < count else EARLY))

    def turn(h, v):
        rows = extent[h]
        return (v * cos_ref[rows] + pltpu.roll(v, HD // 2, 1) * sin_ref[rows]).astype(BF16)

    for h in range(count):
        new = pp[h][chip, :, WIDE:PROJ]
        for p, _ in others:
            arrived(kr[h].at[p], kr_recv[h].at[p])
            new = new + restore(kr[h].at[p], size[h] // 16, 2)
        fresh = pl.ds(pl.multiple_of(CACHE + r * ROWS + PIECES[h][0], 16), size[h])
        kv[fresh, 0:HD] = turn(h, new[:, 0:HD])
        kv[fresh, HD : 2 * HD] = new[:, HD : 2 * HD].astype(BF16)

    def nk_rows(red):
        return kv.at[pl.ds(pl.multiple_of(CACHE + red * ROWS, ROWS), ROWS), 0 : 2 * HD]

    def nk_to(slot, red, to):
        send(nk_rows(red), nk_rows(red), nk_send.at[slot], nk_recv.at[red], to)

    for i, (p, to) in enumerate(others):
        nk_to(i, r, to)
    nk_to(7, r, sibling)
    send_queries(count - 1, range(EARLY, 7))

    for red in (
        red_of(xh, y + 1, c), red_of(xh, y + 3, c), red_of(xh, y + 2, c),
        red_of(1 - xh, y + 1, c), red_of(1 - xh, y + 3, c), red_of(1 - xh, y + 2, c),
    ):
        arrived(kv_rows(red), kv_recv.at[red])
        kv_send_to(red, sibling)

    for k in range(8):
        red = rem(chip + k, 8) * 2 + 1 - c
        arrived(kv_rows(red), kv_recv.at[red])
    turn_log = HD ** (-0.5) * math.log2(math.e)

    def scores(h, n):
        keys = kv[pl.ds(pl.multiple_of(n * CHUNK, CHUNK), CHUNK), 0:HD]
        return lax.dot_general(qh[h][...], keys, (((1,), (1,)), ((), ())), preferred_element_type=F32)

    def keep(h, n, t, top):
        s_ref[h][:, pl.ds(pl.multiple_of(n * CHUNK, CHUNK), CHUNK)] = t
        for k in range(CHUNK // HD):
            top = jnp.maximum(top, t[:, k * HD : (k + 1) * HD])
        return top

    def first_pass(h):
        query = pp[h][chip, :, 0:WIDE]
        for p, _ in others:
            arrived(qr[h].at[p], qr_recv[h].at[p])
            query = query + restore(qr[h].at[p], size[h] // 16, 8)
        for k in range(8):
            qh[h][k * size[h] : (k + 1) * size[h], :] = turn(h, query[:, k * HD : (k + 1) * HD])

        def plain(n, top, h=h):
            return keep(h, n, scores(h, n), top)

        def partly(n, top, h=h):
            slot = n * CHUNK + lax.broadcasted_iota(I32, (1, CHUNK), 1)
            return keep(h, n, scores(h, n) + jnp.where(slot < start, 0.0, NEG), top)

        top = jnp.full((8 * size[h], HD), NEG, F32)
        top = lax.fori_loop(0, 4, plain, top)
        return lax.fori_loop(4, 8, partly, top)

    tops = [first_pass(0)]

    for i, (p, _) in enumerate(nearest):
        red = p * 2 + c
        arrived(nk_rows(red), nk_recv.at[red])
        nk_to(8 + i, red, sibling)
    for k in range(8):
        red = rem(chip + k, 8) * 2 + 1 - c
        arrived(nk_rows(red), nk_recv.at[red])

    at_count = [0] * count

    def at_to(h, red, to):
        send(att[h].at[red], att[h].at[red], at_send[h].at[at_count[h]], at_recv[h].at[red], to)
        at_count[h] += 1

    for h in range(count):
        many = 8 * size[h]
        if h > 0:
            tops.append(first_pass(h))
        token = r * ROWS + PIECES[h][0] + rem(lax.broadcasted_iota(I32, (many, CHUNK), 0), size[h])
        ahead = lax.broadcasted_iota(I32, (many, CHUNK), 1) > token
        top = keep(h, 8, jnp.where(ahead, NEG, scores(h, 8)), tops[h])
        peak = jnp.broadcast_to(jnp.max(top, axis=1, keepdims=True), (many, HD))

        mix[h][...] = jnp.zeros((many, 2 * HD), F32)

        def weigh(n, _, h=h, peak=peak):
            base = n * CHUNK
            parts = []
            for k in range(CHUNK // HD):
                t = s_ref[h][:, pl.ds(pl.multiple_of(base + k * HD, HD), HD)]
                parts.append(jnp.exp2((t - peak) * turn_log).astype(BF16))
            wts = jnp.concatenate(parts, axis=1)
            vals = kv[pl.ds(pl.multiple_of(base, CHUNK), CHUNK), HD : 3 * HD]
            mix[h][...] += jnp.dot(wts, vals, preferred_element_type=F32)
            return 0

        lax.fori_loop(0, 9, weigh, 0)
        done = (mix[h][:, 0:HD] / mix[h][:, HD : 2 * HD]).astype(BF16)
        for k in range(8):
            att[h][r, :, k * HD : (k + 1) * HD] = done[k * size[h] : (k + 1) * size[h], :]
        for p, to in others:
            at_to(h, r, to)
        at_to(h, r, sibling)
    sent(sends[-16:])

    loads[8].wait()

    def project_out(h):
        for p, _ in nearest:
            red = p * 2 + c
            arrived(att[h].at[red], at_recv[h].at[red])
            at_to(h, red, sibling)
        for k in range(8):
            red = rem(chip + k, 8) * 2 + 1 - c
            arrived(att[h].at[red], at_recv[h].at[red])
        for m in range(2):
            x = att[h][m * 8 : (m + 1) * 8].reshape(8 * size[h], WIDE)
            for n in range(WIDE // 256):
                lanes = slice(n * 256, (n + 1) * 256)
                t = jnp.dot(x, wo[:, lanes], preferred_element_type=F32)
                op[h][m * 8 : (m + 1) * 8, :, lanes] = t.reshape(8, size[h], 256)

    def ring(h, stage):
        s = sense[h]
        up, down, over = z_next[s], z_next[-s], z_over[s]

        def own(d):
            return op[h][blk_of(xl, z + s * d)]

        def other(d):
            return op[h][blk_of(ox, z + s * d)]

        def x_send(k, v):
            quantize(xs[h].at[k], v)
            send(xs[h].at[k], xr[h].at[k], xs_send[h].at[k], xr_recv[h].at[k], x_pair)

        def x_get(k):
            arrived(xr[h].at[k], xr_recv[h].at[k])
            return restore(xr[h].at[k], size[h] // 16, 8)

        def z_send(k, v, to):
            quantize(zs[h].at[k], v)
            send(zs[h].at[k], zr[h].at[k], zs_send[h].at[k], zr_recv[h].at[k], to)

        def z_get(k):
            arrived(zr[h].at[k], zr_recv[h].at[k])
            return restore(zr[h].at[k], size[h] // 16, 8)

        if stage == 0:
            x_send(0, other(4))
            z_send(9, other(-2), down)
            x_send(1, other(-3))
            x_send(2, other(3))
            x_send(4, other(2))
        if stage == 1:
            z_send(0, own(4) + x_get(0), up)
            z_send(6, own(-3) + x_get(1), down)
            z_send(5, other(1), up)
        if stage == 2:
            z_send(10, other(-1) + z_get(9), down)
        if stage == 3:
            z_send(1, own(3) + z_get(0) + x_get(2), up)
            z_send(7, own(-2) + z_get(6), down)
        if stage == 4:
            x_send(3, other(0) + z_get(5) + z_get(10))
        if stage == 5:
            z_send(2, own(2) + z_get(1) + x_get(4), up)
            z_send(8, own(-1) + z_get(7), down)
        if stage == 6:
            z_send(3, own(1) + z_get(2), up)
        if stage == 7:
            rows = extent[h]
            out_ref[rows] = res[rows] + (own(0) + x_get(3) + z_get(8) + z_get(3))

    for step in (9, 0, 1, 2, 19, 10, 3, 11, 12, 4, 5, 13, 6, 14, 15, 7, 16, 17):
        if step % 10 == 9:
            project_out(step // 10)
        else:
            ring(step // 10, step % 10)
    sent([])


def on_device(resid, norm_gain, w_query, w_key, w_value, w_out, cache_key, cache_value, prefix_len):
    half = HD // 2
    steps = jnp.arange(HD, dtype=I32)
    steps = jnp.where(steps < half, steps, steps - half).astype(F32)
    freq = (THETA ** (-(steps * 2.0) / HD))[None, :]
    vmem = pl.BlockSpec(memory_space=pltpu.VMEM)
    hbm = pl.BlockSpec(memory_space=pl.ANY)
    dma = pltpu.SemaphoreType.DMA
    scratch = [
        pltpu.VMEM((ROWS, HD), F32),
        pltpu.VMEM((ROWS, HD), F32),
        pltpu.VMEM((ROWS, WIDE), F32),
        pltpu.VMEM((2, WIDE, PROJ), BF16),
        pltpu.VMEM((WIDE, WIDE), BF16),
        pltpu.VMEM((KEYS, 3 * HD), BF16),
        pltpu.VMEM((SLOTS, 2 * HD), BF16),
        pltpu.VMEM((16, 8, HD), F32),
        dma((9,)), dma((2,)), dma((15,)), dma((16,)),
        dma((15,)), dma((16,)), dma((15,)), dma((16,)),
    ]
    for _, n in PIECES:
        few, many = (tiles(n, 2 * HD), 16, HD), (tiles(n, WIDE), 16, HD)
        scratch += [
            pltpu.VMEM((2, 8, n, WIDE), BF16),
            pltpu.VMEM((8, n, WIDE), BF16),
            pltpu.VMEM((8, n, PROJ), F32),
            pltpu.VMEM((7,) + few, I16),
            pltpu.VMEM((8,) + few, I16),
            pltpu.VMEM((7,) + many, I16),
            pltpu.VMEM((8,) + many, I16),
            pltpu.VMEM((8 * n, HD), BF16),
            pltpu.VMEM((8 * n, KEYS), F32),
            pltpu.VMEM((8 * n, 2 * HD), F32),
            pltpu.VMEM((16, n, WIDE), BF16),
            pltpu.VMEM((16, n, WIDE), F32),
            pltpu.VMEM((5,) + many, I16),
            pltpu.VMEM((5,) + many, I16),
            pltpu.VMEM((11,) + many, I16),
            pltpu.VMEM((11,) + many, I16),
            dma((15,)), dma((16,)), dma((8,)), dma((8,)),
            dma((7,)), dma((8,)), dma((7,)), dma((8,)),
            dma((15,)), dma((16,)),
            dma((5,)), dma((5,)), dma((11,)), dma((11,)),
        ]
    return pl.pallas_call(
        kernel,
        out_shape=jax.ShapeDtypeStruct((ROWS, WIDE), F32),
        in_specs=[pl.BlockSpec(memory_space=pltpu.SMEM), hbm, vmem, hbm, hbm, hbm, hbm, hbm, hbm, vmem],
        out_specs=vmem,
        scratch_shapes=scratch,
        compiler_params=pltpu.CompilerParams(
            collective_id=0, has_side_effects=True, vmem_limit_bytes=58 * 1024 * 1024
        ),
    )(prefix_len, resid, norm_gain[None, :], w_query, w_key, w_value, w_out, cache_key, cache_value, freq)


def solution(mesh):
    placed = (
        P("blk", "red"), P("red"), P("red", "blk"), P("red", None), P("red", None), P("blk", "red"),
        P("red", None), P("red", None), P(),
    )
    return jax.shard_map(on_device, mesh=mesh, in_specs=placed, out_specs=P("blk", "red"), check_vma=False)
```

time: 114 us -> 111 us (0.974)
  Pallas kernels: 110 us -> 107 us
    pallas_call x1, Pallas kernels: 110 us -> 107 us  [on_device(): pl.pallas_call(kernel, out_shape=jax.ShapeDtypeStruct((ROWS, WIDE), F32),...]
where the time goes in v3:
time: 111 us; the launch traced here: 110 us
  Pallas kernels  107 us (96%)
  local copies, waits for them, and re-layouts  1.67 us (2%)
    pallas_call x1, Pallas kernels, on_device(): pl.pallas_call(kernel, out_shape=jax.ShapeDtypeStruct((ROWS, WIDE), F32),...  107 us

profile of v3, /device:TPU:32, one launch (start us, length us, event | category | flops | bytes accessed | tf_op | source)
XLA Modules:
  0.0 110.2 jit_solution(14105838123731154682)
XLA Ops:
  0.7 0.5 fusion.4.freq_ref
  1.2 107.3 %shard_map.91 = f32[64,1024]{1,0:T(8,128)} custom-call(s32[1]{0:T(128)S(6)} %copy.11.start_ref, f32[64,1024]{1,0:T(8,128)} %resid_hbm.1, f32[1,1024]{1,0:T(1,128)} %bitcast.1, bf16[1024,1024]{1,0:T(8,128)(2,1)} %wq_hbm.1, bf16[1024,1024]{1,0:T(8,128)(2,1)} %wk_hbm.1, bf16[1024,1024]{1,0:T(8,128)(2,1)} %wv_hbm.1, bf16[1024,1024]{1,0:T(8,128)(2,1)} %wo_hbm.1, ...), custom_call_target="tpu_custom_call" | custom-call | tf_op jit(solution)/shard_map/pallas_call | solution.py:564
  108.5 1.7 %copy.12 = f32[64,1024]{1,0:T(8,128)} copy(f32[64,1024]{1,0:T(8,128)} %shard_map.91) | data formatting | bytes 524288

commit v4 on v3

--- a/solution.py
+++ b/solution.py
@@ -390,8 +390,8 @@
             return keep(h, n, scores(h, n) + jnp.where(slot < start, 0.0, NEG), top)
 
         top = jnp.full((8 * size[h], HD), NEG, F32)
-        top = lax.fori_loop(0, 4, plain, top)
-        return lax.fori_loop(4, 8, partly, top)
+        top = lax.fori_loop(0, 4, plain, top, unroll=2)
+        return lax.fori_loop(4, 8, partly, top, unroll=2)
 
     tops = [first_pass(0)]
 
@@ -431,7 +431,7 @@
             mix[h][...] += jnp.dot(wts, vals, preferred_element_type=F32)
             return 0
 
-        lax.fori_loop(0, 9, weigh, 0)
+        lax.fori_loop(0, 9, weigh, 0, unroll=3)
         done = (mix[h][:, 0:HD] / mix[h][:, HD : 2 * HD]).astype(BF16)
         for k in range(8):
             att[h][r, :, k * HD : (k + 1) * HD] = done[k * size[h] : (k + 1) * size[h], :]

time: 111 us -> 110 us (level)
  Pallas kernels: 107 us -> 105 us
    pallas_call x1, Pallas kernels: 107 us -> 105 us  [on_device(): pl.pallas_call(kernel, out_shape=jax.ShapeDtypeStruct((ROWS, WIDE), F32),...]
where the time goes in v4:
time: 110 us; the launch traced here: 108 us
  Pallas kernels  105 us (95%)
  local copies, waits for them, and re-layouts  1.67 us (2%)
    pallas_call x1, Pallas kernels, on_device(): pl.pallas_call(kernel, out_shape=jax.ShapeDtypeStruct((ROWS, WIDE), F32),...  105 us

profile of v4, /device:TPU:32, one launch (start us, length us, event | category | flops | bytes accessed | tf_op | source)
XLA Modules:
  0.0 108.1 jit_solution(12263565262703924683)
XLA Ops:
  0.7 0.5 fusion.4.freq_ref
  1.2 105.3 %shard_map.91 = f32[64,1024]{1,0:T(8,128)} custom-call(s32[1]{0:T(128)S(6)} %copy.11.start_ref, f32[64,1024]{1,0:T(8,128)} %resid_hbm.1, f32[1,1024]{1,0:T(1,128)} %bitcast.1, bf16[1024,1024]{1,0:T(8,128)(2,1)} %wq_hbm.1, bf16[1024,1024]{1,0:T(8,128)(2,1)} %wk_hbm.1, bf16[1024,1024]{1,0:T(8,128)(2,1)} %wv_hbm.1, bf16[1024,1024]{1,0:T(8,128)(2,1)} %wo_hbm.1, ...), custom_call_target="tpu_custom_call" | custom-call | tf_op jit(solution)/shard_map/pallas_call | solution.py:564
  106.5 1.7 %copy.12 = f32[64,1024]{1,0:T(8,128)} copy(f32[64,1024]{1,0:T(8,128)} %shard_map.91) | data formatting | bytes 524288
